TPU v7x, 32 devices: a whole 2x2x4 slice. The times are simulated.
32 devices in a mesh: ctx: 32 (over z, y, x, core), exp: 1.
Axes of the slice: x: 2, y: 2, z: 4, core: 2. Of those that a mesh axis runs over, the one named last changes fastest.
Arguments:
- tokens: bfloat16 [4096, 2880], P('ctx', 'exp'), may hold values from -6 to 6
- route_ids: int32 [4096, 4], P('ctx'), may hold values from 0 to 31, all different within a row; in each aligned block of 128 rows (0 to 127, 128 to 255, ...) at most 20 rows name the same one
- combine: float32 [4096, 4], P('ctx'), may hold values from 0.05 to 0.6
- gain_attn: float32 [2880], replicated, may hold values from 0.25 to 1.75
- gain_moe: float32 [2880], replicated, may hold values from 0.25 to 1.75
- query_weight: bfloat16 [2880, 4096], P(None, ('exp', 'ctx'))
- key_weight: bfloat16 [2880, 512], P(None, ('exp', 'ctx')), may hold values from -0.109375 to 0.109375
- value_weight: bfloat16 [2880, 512], P(None, ('exp', 'ctx')), may hold values from -0.109375 to 0.109375
- attn_sinks: float32 [64], P('exp'), may hold values from 1 to 6
- out_weight: bfloat16 [4096, 2880], P('exp', 'ctx'), may hold values from -0.09375 to 0.09375
- gate_up_weight: bfloat16 [32, 2, 2880, 2880], P('ctx', None, None, 'exp'), may hold values from -0.109375 to 0.109375
- down_weight: bfloat16 [32, 2880, 2880], P('ctx', 'exp'), may hold values from -0.109375 to 0.109375
Outputs:
- layer_out: bfloat16 [4096, 2880], P('ctx', 'exp')
Inputs may be any that keep to these rules, and one draw needn't show every extreme that they name: `route_ids`: in each aligned block of 128 rows (the tokens of one index of ctx) no expert is named by more than 20 rows, a bound that some block reaches.
All inputs are finite; a program needn't handle non-finite values.
Results may differ from a plain program's by a relative error of at most 0.02.
Values may be sent and summed in bfloat16 or wider, within the bound.
No kernel may reach another device: no remote copies, remote signals or barrier semaphores. Data moves between devices by JAX's collectives and lax.ppermute only.
A program may use at most 256 MiB of HBM per device.

v0:
```python
import functools
import math

import jax
import jax.numpy as jnp
from jax import lax
from jax.experimental import pallas as pl
from jax.experimental.pallas import tpu as pltpu
from jax.sharding import PartitionSpec as P

HD = 64
WINDOW = 128
EPSILON = 1e-05
ROPE_BASE = 150000.0
PLANE = 8
BF16 = jnp.bfloat16
F32 = jnp.float32


def rms_norm(values, gain):
    wide = values.astype(F32)
    meansq = jnp.mean(wide * wide, axis=-1, keepdims=True)
    return (wide * lax.rsqrt(meansq + EPSILON) * gain).astype(BF16)


def rms_norm_t(values, gain):
    wide = values.astype(F32)
    meansq = jnp.mean(wide * wide, axis=0, keepdims=True)
    return (wide * lax.rsqrt(meansq + EPSILON) * gain[:, None]).astype(BF16)


def rotary(values, angles_pos):
    half_dim = values.shape[-1] // 2
    inverse_freq = jnp.exp(
        -(2.0 * jnp.arange(half_dim, dtype=F32) / values.shape[-1]) * math.log(ROPE_BASE)
    )
    angles = angles_pos[:, None] * inverse_freq[None, :]
    cosine = jnp.cos(angles)[:, None, :]
    sine_part = jnp.sin(angles)[:, None, :]
    first_half = values[..., :half_dim]
    second_half = values[..., half_dim:]
    return jnp.concatenate(
        [
            first_half * cosine - second_half * sine_part,
            second_half * cosine + first_half * sine_part,
        ],
        axis=-1,
    )


def sink_softmax(scores, key_mask, sink_col):
    masked = jnp.where(key_mask, scores, -1e30)
    row_top = jnp.maximum(jnp.max(masked, axis=-1, keepdims=True), sink_col)
    weights = jnp.where(key_mask, jnp.exp(masked - row_top), 0.0)
    denominator = jnp.sum(weights, axis=-1, keepdims=True) + jnp.exp(sink_col - row_top)
    return (weights / denominator).astype(BF16)


def attend_block(query_rows, key_rows, value_rows, query_pos, key_pos, sink_col):
    scores = jnp.einsum(
        "qkgd,skd->kgqs", query_rows, key_rows, preferred_element_type=F32
    ) * HD ** (-0.5)
    distance = query_pos[:, None] - key_pos[None, :]
    key_mask = (distance >= 0) & (distance < WINDOW) & (key_pos >= 0)[None, :]
    weights = sink_softmax(scores, key_mask, sink_col)
    mixed_rows = jnp.einsum("kgqs,skd->qkgd", weights, value_rows, preferred_element_type=F32)
    return mixed_rows.astype(BF16).reshape(query_rows.shape[0], -1)


def dot32(a, b):
    return jnp.dot(a, b, preferred_element_type=F32)


def project_whole(tokens, gain_attn, query_weight, key_weight, value_weight, attn_sinks, out_weight):
    tok_dev = tokens.shape[0]
    full_rows = lax.all_gather(tokens, "exp", axis=1, tiled=True)
    normed = rms_norm(full_rows, gain_attn)
    pieces = lax.all_gather((query_weight, key_weight, value_weight), "ctx", axis=1, tiled=True)
    query_lin, key_lin, value_lin = tuple(dot32(normed, piece) for piece in pieces)
    heads_local = query_lin.shape[1] // HD
    kv_local = key_lin.shape[1] // HD
    group_size = heads_local // kv_local
    position_ids = lax.axis_index("ctx") * tok_dev + jnp.arange(tok_dev, dtype=jnp.int32)
    angles_pos = position_ids.astype(F32)
    query = rotary(query_lin.reshape(tok_dev, heads_local, HD), angles_pos).astype(BF16)
    keys_own = rotary(key_lin.reshape(tok_dev, kv_local, HD), angles_pos).astype(BF16)
    key_value = jnp.stack([keys_own.reshape(tok_dev, kv_local * HD), value_lin.astype(BF16)])
    n_ctx = lax.axis_size("ctx")
    previous = lax.ppermute(key_value, "ctx", [(i, i + 1) for i in range(n_ctx - 1)])
    context = jnp.concatenate([previous, key_value], axis=1)
    key_pos = position_ids[0] - WINDOW + jnp.arange(tok_dev + WINDOW, dtype=jnp.int32)
    attended = attend_block(
        query.reshape(tok_dev, kv_local, group_size, HD),
        context[0].reshape(-1, kv_local, HD),
        context[1].reshape(-1, kv_local, HD),
        position_ids,
        key_pos,
        attn_sinks.reshape(kv_local, group_size, 1, 1),
    )
    head_terms = dot32(attended, lax.all_gather(out_weight, "ctx", axis=1, tiled=True))
    attn_proj = lax.psum(head_terms.astype(BF16), "exp").astype(F32)
    return (full_rows.astype(F32) + attn_proj).astype(BF16).T


def dot_nt(a, b):
    return lax.dot_general(a, b, (((1,), (1,)), ((), ())), preferred_element_type=F32)


def turn(values, cosine, signed_sine):
    width = values.shape[1]
    half = HD // 2
    lane = lax.broadcasted_iota(jnp.int32, values.shape, 1) % HD
    partner = jnp.where(
        lane < half,
        pltpu.roll(values, width - half, 1),
        pltpu.roll(values, half, 1),
    )
    return values * cosine + partner * signed_sine


def qkv_kernel(count, *refs):
    blocks, refs = refs[:count], refs[count:]
    weight_ref, cos_ref, sin_ref, q_ref, key_value_ref, rows_ref, kv_ref = refs
    step = pl.program_id(0)
    width, rows = blocks[0].shape
    cols = weight_ref.shape[2]
    share = kv_ref.shape[2]

    @pl.when(step == 0)
    def _():
        for r in range(count):
            rows_ref[r * rows : (r + 1) * rows, :] = blocks[r][...].T

    for i in range(2):
        for tile in range(-(-width // cols)):
            at, lanes = width + 2 * share * tile, slice(tile * cols, (tile + 1) * cols)
            for part in range(2):
                kv_ref[part, 2 * step + i, :, lanes] = weight_ref[i, at + part * share : at + (part + 1) * share]

    weight = jnp.concatenate([weight_ref[0, :width], weight_ref[1, :width]], axis=1)
    query = dot32(rows_ref[...], weight)
    for r in range(count):
        for at in range(0, 2 * cols, cols):
            piece = query[r * rows : (r + 1) * rows, at : at + cols]
            q_ref[r, :, at : at + cols] = turn(piece, cos_ref[r], sin_ref[r]).astype(BF16)

    @pl.when(step == pl.num_programs(0) - 1)
    def _():
        both = kv_ref[...].reshape(2 * PLANE * share, kv_ref.shape[3])[:, :width]
        lines = dot_nt(rows_ref[...], both)
        half = PLANE * share
        for r in range(count):
            piece = lines[r * rows : (r + 1) * rows]
            key_value_ref[r, :, :half] = turn(piece[:, :half], cos_ref[r], sin_ref[r]).astype(BF16)
            key_value_ref[r, :, half:] = piece[:, half:].astype(BF16)


def project_blocks(blocks, weights, share, cosine, signed_sine):
    count = len(blocks)
    width, rows = blocks[0].shape
    cols = weights.shape[2]
    tiles = -(-width // cols)
    kv_cols = 2 * PLANE * share
    whole = lambda p: (0, 0, 0)
    return pl.pallas_call(
        functools.partial(qkv_kernel, count),
        grid=(PLANE // 2,),
        in_specs=[pl.BlockSpec((width, rows), lambda p: (0, 0))] * count
        + [
            pl.BlockSpec((2,) + weights.shape[1:], lambda p: (p, 0, 0)),
            pl.BlockSpec(cosine.shape, whole),
            pl.BlockSpec(signed_sine.shape, whole),
        ],
        out_specs=[
            pl.BlockSpec((count, rows, 2 * cols), lambda p: (0, 0, p)),
            pl.BlockSpec((count, rows, kv_cols), whole),
        ],
        out_shape=[
            jax.ShapeDtypeStruct((count, rows, PLANE * cols), BF16),
            jax.ShapeDtypeStruct((count, rows, kv_cols), BF16),
        ],
        scratch_shapes=[
            pltpu.VMEM((count * rows, width), BF16),
            pltpu.VMEM((2, PLANE, share, tiles * cols), BF16),
        ],
        compiler_params=pltpu.CompilerParams(vmem_limit_bytes=58 * 2**20),
        cost_estimate=pl.CostEstimate(
            flops=2 * count * rows * width * (PLANE * cols + kv_cols),
            bytes_accessed=2 * width * (PLANE * cols + kv_cols + count * rows),
            transcendentals=0,
        ),
    )(*blocks, weights, cosine, signed_sine)


def attend_kernel(
    r, place_ref, sinks_ref, queries_ref, key_values_ref, halos_ref, even_ref, odd_ref, out_ref, att_ref, total_ref
):
    q_ref, own_ref, previous_ref = queries_ref.at[r], key_values_ref.at[r], halos_ref.at[place_ref[1]]
    rows = q_ref.shape[0]
    pair = 2 * HD
    kv_heads = own_ref.shape[1] // pair
    kv_cols = kv_heads * HD
    pairs = q_ref.shape[1] // pair
    lane = lax.broadcasted_iota(jnp.int32, (rows, pair), 1)
    low = lane < HD

    def spread(values, head):
        moved = pltpu.roll(values.astype(F32), HD, 1)
        chunk = values.astype(F32)
        lower, upper = (chunk, moved) if head % 2 == 0 else (moved, chunk)
        zero = jnp.zeros_like(chunk)
        return jnp.concatenate(
            [jnp.where(low, lower, zero), jnp.where(low, zero, upper)], axis=0
        ).astype(BF16)

    def side(ref):
        tables = []
        for head in range(kv_heads):
            at = head // 2 * pair
            keys = spread(ref[:, at : at + pair], head)
            values = spread(ref[:, kv_cols + at : kv_cols + at + pair], head)
            tables.append((keys, values))
        return tables

    own, previous = side(own_ref), side(previous_ref)
    row = lax.broadcasted_iota(jnp.int32, (rows, rows), 0)
    col = lax.broadcasted_iota(jnp.int32, (rows, rows), 1)
    inside = col <= row
    shown = jnp.logical_or(inside, place_ref[0] == 0)
    scale = HD**-0.5
    for p in range(pairs):
        head = p * kv_heads // pairs
        chunk = q_ref[:, p * pair : (p + 1) * pair]
        scores_own = dot_nt(chunk, own[head][0])
        scores_previous = dot_nt(chunk, previous[head][0])
        probs_own, probs_previous = [], []
        for h in range(2):
            at = h * rows
            scores = jnp.where(
                inside, scores_own[:, at : at + rows], scores_previous[:, at : at + rows]
            ) * scale
            scores = jnp.where(shown, scores, -1e30)
            sink = sinks_ref[2 * p + h]
            top = jnp.maximum(jnp.max(scores, axis=1, keepdims=True), sink)
            weights = jnp.exp(scores - top)
            total = jnp.sum(weights, axis=1, keepdims=True) + jnp.exp(sink - top)
            probs = weights / total
            probs_own.append(jnp.where(inside, probs, 0.0).astype(BF16))
            probs_previous.append(jnp.where(inside, 0.0, probs).astype(BF16))
        mixed = dot32(jnp.concatenate(probs_own, axis=1), own[head][1])
        mixed = mixed + dot32(jnp.concatenate(probs_previous, axis=1), previous[head][1])
        att_ref[:, p * pair : (p + 1) * pair] = mixed.astype(BF16)

    half, groups, padded, depth = even_ref.shape
    cols = out_ref.shape[0] // (2 * half * groups)
    attended = att_ref[...]
    for side_at, weight_ref in enumerate((even_ref, odd_ref)):
        for i in range(half):
            terms = dot_nt(weight_ref[i].reshape(groups * padded, depth), attended)
            share = place_ref[2 + 2 * i + side_at]
            for g in range(groups):
                total_ref[g, share] = terms[g * padded : (g + 1) * padded]
    for g in range(groups):
        for p in range(2 * half):
            at = (g * 2 * half + p) * cols
            out_ref[at : at + cols, :] = total_ref[g, p, :cols, :]


def attend_and_project(r, place, sinks, queries, key_values, halos, even, odd, width):
    rows = queries.shape[1]
    half, groups, padded, depth = even.shape
    vmem = pl.BlockSpec(memory_space=pltpu.VMEM)
    smem = pl.BlockSpec(memory_space=pltpu.SMEM)
    return pl.pallas_call(
        functools.partial(attend_kernel, r),
        in_specs=[smem, smem] + [vmem] * 5,
        out_specs=vmem,
        out_shape=jax.ShapeDtypeStruct((width, rows), F32),
        scratch_shapes=[
            pltpu.VMEM((rows, depth), BF16),
            pltpu.VMEM((groups, 2 * half, padded, rows), F32),
        ],
        compiler_params=pltpu.CompilerParams(vmem_limit_bytes=40 * 2**20),
        cost_estimate=pl.CostEstimate(
            flops=2 * rows * depth * (width + 8 * rows),
            bytes_accessed=2 * (width * depth + 2 * width * rows),
            transcendentals=rows * rows * depth // HD,
        ),
    )(place, sinks, queries, key_values, halos, even, odd)


def project_planes(tokens, gain_attn, query_weight, key_weight, value_weight, attn_sinks, out_weight):
    tok_dev, width = tokens.shape
    n_ctx = lax.axis_size("ctx")
    n_z = n_ctx // PLANE
    index = lax.axis_index("ctx")
    z, j = index // PLANE, index % PLANE
    planes = [[PLANE * a + b for b in range(PLANE)] for a in range(n_z)]
    order = list(range(0, n_z, 2)) + list(range(1, n_z, 2))[::-1]
    place_of = [order.index(a) for a in range(n_z)]
    ring, places = jnp.array(order, jnp.int32), jnp.array(place_of, jnp.int32)

    def shift(block, steps):
        return lax.ppermute(block, "ctx", [(i, (i + steps * PLANE) % n_ctx) for i in range(n_ctx)])

    def pass_on(block):
        route = [
            (a * PLANE + b, order[place_of[a] - 1] * PLANE + b) for a in range(n_z) for b in range(PLANE)
        ]
        return lax.ppermute(block, "ctx", route)

    def behind(block):
        route = [(a * PLANE + b, a * PLANE + (b + 1) % PLANE) for a in range(n_z) for b in range(PLANE)]
        return lax.ppermute(block, "ctx", route)

    def swap(block, bits):
        return lax.ppermute(block, "ctx", [(i, i ^ bits) for i in range(n_ctx)])

    tokens_t = tokens.T
    blocks = [rms_norm_t(tokens_t, gain_attn)]

    lanes = query_weight.shape[1]
    share = key_weight.shape[1]
    tiles = -(-width // lanes)
    kv_rows = jnp.concatenate([key_weight.T, value_weight.T], axis=0)
    kv_rows = jnp.pad(kv_rows, ((0, 0), (0, tiles * lanes - width))).reshape(2 * share, tiles, lanes)
    packed = jnp.concatenate(
        [query_weight, kv_rows.transpose(1, 0, 2).reshape(tiles * 2 * share, lanes)], axis=0
    )
    weights = lax.all_gather(packed, "ctx", axis_index_groups=planes)

    cols = out_weight.shape[1]
    padded = -(-cols // 16) * 16
    group_rows = out_weight.shape[0] // n_z
    out_rows = jnp.pad(out_weight.T, ((0, padded - cols), (0, 0)))
    out_rows, blocks[0] = lax.optimization_barrier((out_rows, blocks[0]))
    blocks.append(pass_on(blocks[0]))
    out_groups = jnp.stack(jnp.split(out_rows, n_z, axis=1))
    pieces = [
        shift(lax.dynamic_index_in_dim(out_groups, (z + s) % n_z, 0, keepdims=False), s) if s
        else lax.dynamic_index_in_dim(out_groups, z, 0, keepdims=False)
        for s in range(n_z)
    ]
    ordered = jnp.stack(pieces[::-1] + pieces[:0:-1])
    out_mine = lax.dynamic_slice_in_dim(ordered, n_z - 1 - z, n_z, 0)
    out_mine, blocks[1] = lax.optimization_barrier((out_mine, blocks[1]))
    for _ in range(n_z - 2):
        blocks.append(pass_on(blocks[-1]))
    out_parts = [out_mine] + [swap(out_mine, bits) for bits in (2, 4, 6)]
    out_parts, blocks[-1] = lax.optimization_barrier((out_parts, blocks[-1]))
    out_half = jnp.stack(out_parts)
    out_other = swap(out_half, 1)

    heads = PLANE * query_weight.shape[1] // HD
    sinks = lax.dynamic_slice_in_dim(attn_sinks, z * heads, heads)
    own_rows = jnp.arange(tok_dev, dtype=jnp.int32)
    lane = jnp.arange(2 * HD, dtype=jnp.int32) % HD
    half = HD // 2
    inverse_freq = jnp.exp(-(2.0 * (lane % half).astype(F32) / HD) * math.log(ROPE_BASE))
    mine = places[z]
    block_z = ring[(mine + jnp.arange(n_z, dtype=jnp.int32)) % n_z]
    numbers = block_z * PLANE + j
    angles = (numbers[:, None] * tok_dev + own_rows[None, :]).astype(F32)[:, :, None] * inverse_freq
    signed_sine = jnp.where(lane < half, -jnp.sin(angles), jnp.sin(angles))
    queries, key_values = project_blocks(blocks, weights, share, jnp.cos(angles), signed_sine)
    halos = behind(key_values)
    below = (places[jnp.maximum(block_z - 1, 0)] - mine) % n_z
    previous_at = jnp.where(j == 0, below, jnp.arange(n_z, dtype=jnp.int32))

    relative = jnp.arange(PLANE, dtype=jnp.int32) ^ j
    partial_sums = []
    for r in list(range(1, n_z)) + [0]:
        first = (numbers[r] == 0).astype(jnp.int32)
        place = jnp.concatenate([jnp.stack([first, previous_at[r]]), relative])
        partial_sums.append(
            attend_and_project(
                r, place, sinks, queries, key_values, halos, out_half, out_other, width
            )
        )
    running = partial_sums[0].astype(BF16)
    for term in partial_sums[1:]:
        running = pass_on(running).astype(F32) + term
        if term is not partial_sums[-1]:
            running = running.astype(BF16)
    return (tokens_t.astype(F32) + running).astype(BF16)


def expert_kernel(tile, hidden, rows_ref, gate_ref, upper_ref, down_ref, out_ref, total_ref):
    step = pl.program_id(0)
    steps = pl.num_programs(0)

    def add(count, initial):
        rows = rows_ref[...]
        gate = dot32(rows, gate_ref[0, :, :count])
        upper = dot32(rows, upper_ref[0, :, :count])
        activation = (gate * jax.nn.sigmoid(1.702 * gate) * (upper + 1.0)).astype(BF16)
        terms = dot32(activation, down_ref[:count, :])
        total_ref[...] = terms if initial else total_ref[...] + terms

    last = hidden - (-(-hidden // tile) - 1) * tile

    @pl.when(step == 0)
    def _():
        add(tile, True)

    @pl.when(jnp.logical_and(step > 0, step < steps - 1))
    def _():
        add(tile, False)

    @pl.when(step == steps - 1)
    def _():
        add(last, False)
        out_ref[...] = total_ref[...].astype(BF16)


def run_expert(rows, gate_up, down):
    count, width = rows.shape
    hidden = down.shape[0]
    tile = 512 if hidden > 1024 else 256
    return pl.pallas_call(
        functools.partial(expert_kernel, tile, hidden),
        grid=(-(-hidden // tile),),
        in_specs=[
            pl.BlockSpec((count, width), lambda f: (0, 0)),
            pl.BlockSpec((1, width, tile), lambda f: (0, 0, f)),
            pl.BlockSpec((1, width, tile), lambda f: (1, 0, f)),
            pl.BlockSpec((tile, width), lambda f: (f, 0)),
        ],
        out_specs=pl.BlockSpec((count, width), lambda f: (0, 0)),
        out_shape=jax.ShapeDtypeStruct((count, width), BF16),
        scratch_shapes=[pltpu.VMEM((count, width), F32)],
        compiler_params=pltpu.CompilerParams(vmem_limit_bytes=52 * 2**20),
        cost_estimate=pl.CostEstimate(
            flops=6 * count * width * hidden,
            bytes_accessed=6 * width * hidden + 4 * count * width,
            transcendentals=count * hidden,
        ),
    )(rows, gate_up, gate_up, down)


def slot_chunks(capacity):
    first = min(8, capacity)
    return [first, capacity - first] if capacity > first else [first]


def dispatch_kernel(chosen_ref, normed_ref, out_ref):
    out_ref[...] = dot_nt(chosen_ref[...], normed_ref[...]).astype(BF16)


def dispatch(chosen, normed):
    total, rows = chosen.shape
    width = normed.shape[0]
    return pl.pallas_call(
        dispatch_kernel,
        out_shape=jax.ShapeDtypeStruct((total, width), BF16),
        compiler_params=pltpu.CompilerParams(vmem_limit_bytes=24 * 2**20),
        cost_estimate=pl.CostEstimate(
            flops=2 * total * rows * width, bytes_accessed=2 * width * (total + rows), transcendentals=0
        ),
    )(chosen, normed)


def routing(route_ids, combine, n_ctx, capacity):
    tok_dev = route_ids.shape[0]
    named = route_ids[:, :, None] == jnp.arange(n_ctx, dtype=jnp.int32)[None, None, :]
    member = jnp.any(named, axis=1)
    weight_of = jnp.sum(jnp.where(named, combine[:, :, None], 0.0), axis=1)
    rows = jnp.arange(tok_dev, dtype=jnp.int32)
    earlier = (rows[:, None] > rows[None, :]).astype(BF16)
    slot_of = dot32(earlier, member.astype(BF16)).astype(jnp.int32)
    slot_of = jnp.where(member, slot_of, -1).T
    weight_of = weight_of.T
    chunks = []
    first = 0
    for size in slot_chunks(capacity):
        slots = first + jnp.arange(size, dtype=jnp.int32)
        chosen = (slot_of[:, None, :] == slots[None, :, None]).reshape(n_ctx * size, tok_dev)
        scale = jnp.where(chosen, jnp.repeat(weight_of, size, axis=0), 0.0)
        high = scale.astype(BF16)
        low = (scale - high.astype(F32)).astype(BF16)
        chunks.append((size, chosen.astype(BF16), jnp.concatenate([high, low], axis=1)))
        first += size
    return chunks


def mix_experts(normed, chunks, gate_up, down):
    width, tok_dev = normed.shape
    n_ctx, n_exp = lax.axis_size("ctx"), lax.axis_size("exp")
    width_local = width // n_exp

    def tiles(rows, size):
        if size % 8 == 0 or size % 4:
            return rows.reshape(n_ctx, size, -1)
        return rows.reshape(n_ctx, size // 4, 4, -1)

    def exchange(parts):
        return lax.all_to_all(parts, "ctx", split_axis=0, concat_axis=0, tiled=True)

    def in_order(parts, earlier):
        return lax.optimization_barrier((parts, earlier))

    outgoing, received = [], []
    for size, chosen, _ in chunks:
        if outgoing:
            chosen, outgoing[-1] = in_order(chosen, outgoing[-1])
        outgoing.append(tiles(dispatch(chosen, normed), size))
    for parts in outgoing:
        if received:
            parts, received[-1] = in_order(parts, received[-1])
        received.append(exchange(parts))

    results = []
    for i, (size, _, _) in enumerate(chunks):
        if results:
            received[i], results[-1] = in_order(received[i], results[-1])
        rows_in = received[i].reshape(n_ctx * size, width)
        results.append(tiles(run_expert(rows_in, gate_up, down), size))

    answers = []
    for parts in results:
        if answers:
            parts, answers[-1] = in_order(parts, answers[-1])
        answers.append(exchange(parts))

    moe_out = jnp.zeros((width_local, tok_dev), F32)
    for (size, _, scale), answer in zip(chunks, answers):
        if n_exp > 1:
            answer = lax.psum_scatter(answer, "exp", scatter_dimension=answer.ndim - 1, tiled=True)
        terms = lax.dot_general(
            answer.reshape(n_ctx * size, width_local), scale, (((0,), (0,)), ((), ())),
            preferred_element_type=F32,
        )
        moe_out = moe_out + terms[:, :tok_dev] + terms[:, tok_dev:]
    return moe_out


def per_device(
    tokens,
    route_ids,
    combine,
    gain_attn,
    gain_moe,
    query_weight,
    key_weight,
    value_weight,
    attn_sinks,
    out_weight,
    gate_up_weight,
    down_weight,
):
    tok_dev, width_local = tokens.shape
    n_ctx = lax.axis_size("ctx")
    n_exp = lax.axis_size("exp")
    capacity = tok_dev * route_ids.shape[1] * 5 // (4 * n_ctx)
    chunks = routing(route_ids, combine, n_ctx, capacity)
    by_planes = n_exp == 1 and n_ctx % PLANE == 0 and n_ctx > PLANE
    project = project_planes if by_planes else project_whole
    residual = project(
        tokens, gain_attn, query_weight, key_weight, value_weight, attn_sinks, out_weight
    )
    width = residual.shape[0]
    normed_moe = rms_norm_t(residual, gain_moe)
    exp_index = lax.axis_index("exp")
    residual_local = lax.dynamic_slice_in_dim(residual, exp_index * width_local, width_local, 0)

    moe_out = mix_experts(normed_moe, chunks, gate_up_weight[0], down_weight[0])
    return (residual_local.astype(F32) + moe_out).astype(BF16).T


def solution(mesh):
    return jax.shard_map(
        per_device,
        mesh=mesh,
        in_specs=(
            P("ctx", "exp"),
            P("ctx", None),
            P("ctx", None),
            P(),
            P(),
            P(None, ("exp", "ctx")),
            P(None, ("exp", "ctx")),
            P(None, ("exp", "ctx")),
            P("exp"),
            P("exp", "ctx"),
            P("ctx", None, None, "exp"),
            P("ctx", "exp", None),
        ),
        out_specs=P("ctx", "exp"),
        check_vma=False,
    )
```

profile of v0, /device:TPU:0, one launch (start us, length us, event | category | flops | bytes accessed | tf_op | source)
XLA Modules:
  0.0 417.7 jit_solution(7759632345542918010)
XLA Ops:
  11.1 5.1 %collective-permute-start = (bf16[96,1024]{1,0:T(8,128)(2,1)S(1)}, bf16[96,1024]{1,0:T(8,128)(2,1)S(1)}, u32[]{:S(2)}, u32[]{:S(2)}) collective-permute-start(bf16[96,1024]{1,0:T(8,128)(2,1)S(1)} %get-tuple-element.51), channel_id=1, source_target_pairs={{0,24},{1,25},{2,26},{3,27},{4,28},{5,29},{6,30},{7,31},{8,0},{9,1... | collective-permute-start | bytes 589832 | tf_op jit(solution)/shard_map/ppermute | solution.py:304
  17.2 3.4 collective-permute-start.3
  21.5 12.3 %collective-permute-done.1 = bf16[96,1024]{1,0:T(8,128)(2,1)S(1)} collective-permute-done((bf16[96,1024]{1,0:T(8,128)(2,1)S(1)}, bf16[96,1024]{1,0:T(8,128)(2,1)S(1)}, u32[]{:S(2)}, u32[]{:S(2)}) %collective-permute-start.1) | collective-permute-done | bytes 196640 | tf_op jit(solution)/shard_map/ppermute | solution.py:304
  34.0 14.8 %collective-permute-done.3.refs_1_ = bf16[2880,128]{1,0:T(8,128)(2,1)} collective-permute-done((bf16[2880,128]{1,0:T(8,128)(2,1)S(1)}, bf16[2880,128]{1,0:T(8,128)(2,1)}, u32[]{:S(2)}, u32[]{:S(2)}) %collective-permute-start.3) | collective-permute-done | bytes 737312 | tf_op jit(solution)/shard_map/ppermute | solution.py:310
  48.8 2.4 collective-permute-start.7
  52.3 15.2 %collective-permute-done.4.refs_2_ = bf16[2880,128]{1,0:T(8,128)(2,1)S(1)} collective-permute-done((bf16[2880,128]{1,0:T(8,128)(2,1)}, bf16[2880,128]{1,0:T(8,128)(2,1)S(1)}, u32[]{:S(2)}, u32[]{:S(2)}) %collective-permute-start.4) | collective-permute-done | bytes 737312 | tf_op jit(solution)/shard_map/ppermute | solution.py:310
  67.5 11.2 %collective-permute-done.7 = bf16[4,96,1024]{2,1,0:T(8,128)(2,1)S(1)} collective-permute-done((bf16[4,96,1024]{2,1,0:T(8,128)(2,1)S(1)}, bf16[4,96,1024]{2,1,0:T(8,128)(2,1)S(1)}, u32[]{:S(2)}, u32[]{:S(2)}) %collective-permute-start.7) | collective-permute-done | bytes 786464 | tf_op jit(solution)/shard_map/ppermute | solution.py:317
  78.6 15.3 %collective-permute-done.6 = bf16[4,96,1024]{2,1,0:T(8,128)(2,1)S(1)} collective-permute-done((bf16[4,96,1024]{2,1,0:T(8,128)(2,1)S(1)}, bf16[4,96,1024]{2,1,0:T(8,128)(2,1)S(1)}, u32[]{:S(2)}, u32[]{:S(2)}) %collective-permute-start.6) | collective-permute-done | bytes 786464 | tf_op jit(solution)/shard_map/ppermute | solution.py:317
  101.3 10.7 %shard_map.136 = (bf16[4,128,1024]{2,1,0:T(8,128)(2,1)}, bf16[4,128,256]{2,1,0:T(8,128)(2,1)}) custom-call(bf16[2880,128]{1,0:T(8,128)(2,1)} %copy-done.19, bf16[2880,128]{1,0:T(8,128)(2,1)} %collective-permute-done.3.refs_1_, bf16[2880,128]{1,0:T(8,128)(2,1)} %copy-done.27, bf16[2880,128]{1,0:T(8,128)(2,1)} %copy-done.28, bf16[8,3616,128]{2,1,0:T(8,128)(2,1)} %bitcast.102, ...), custom_call_target="tpu_custom_call" | custom-call | flops 3774873600 | bytes 10321920 | tf_op jit(solution)/shard_map/pallas_call | solution.py:165
  115.0 2.0 add_add_fusion
  121.1 6.6 %shard_map.137 = f32[2880,128]{1,0:T(8,128)S(1)} custom-call(s32[10]{0:T(128)S(1)} %get-tuple-element.58.place_ref, f32[16]{0:T(128)S(1)} %dynamic_slice.24.sinks_ref, bf16[4,128,1024]{2,1,0:T(8,128)(2,1)S(1)} %copy-done, bf16[4,128,256]{2,1,0:T(8,128)(2,1)S(1)} %copy-done.3, bf16[4,128,256]{2,1,0:T(8,128)(2,1)S(1)} %collective-permute-done.9.halos_ref, ...), custom_call_target="tpu_custom_call" | custom-call | flops 1023410176 | bytes 7372800 | tf_op jit(solution)/shard_map/pallas_call | solution.py:274
  129.6 6.6 %shard_map.138 = f32[2880,128]{1,0:T(8,128)S(1)} custom-call(s32[10]{0:T(128)S(1)} %get-tuple-element.59.place_ref, f32[16]{0:T(128)S(1)} %dynamic_slice.24.sinks_ref, bf16[4,128,1024]{2,1,0:T(8,128)(2,1)S(1)} %copy-done, bf16[4,128,256]{2,1,0:T(8,128)(2,1)S(1)} %copy-done.3, bf16[4,128,256]{2,1,0:T(8,128)(2,1)S(1)} %collective-permute-done.9.halos_ref, ...), custom_call_target="tpu_custom_call" | custom-call | flops 1023410176 | bytes 7372800 | tf_op jit(solution)/shard_map/pallas_call | solution.py:274
  136.3 10.6 %collective-permute-done.11 = bf16[2880,128]{1,0:T(8,128)(2,1)S(1)} collective-permute-done((bf16[2880,128]{1,0:T(8,128)(2,1)S(1)}, bf16[2880,128]{1,0:T(8,128)(2,1)S(1)}, u32[]{:S(2)}, u32[]{:S(2)}) %collective-permute-start.11) | collective-permute-done | bytes 737312 | tf_op jit(solution)/shard_map/ppermute | solution.py:310
  154.1 6.6 %shard_map.139 = f32[2880,128]{1,0:T(8,128)S(1)} custom-call(s32[10]{0:T(128)S(1)} %get-tuple-element.60.place_ref, f32[16]{0:T(128)S(1)} %dynamic_slice.24.sinks_ref, bf16[4,128,1024]{2,1,0:T(8,128)(2,1)S(1)} %copy-done.1, bf16[4,128,256]{2,1,0:T(8,128)(2,1)S(1)} %copy-done.4, bf16[4,128,256]{2,1,0:T(8,128)(2,1)S(1)} %copy-done.6, ...), custom_call_target="tpu_custom_call" | custom-call | flops 1023410176 | bytes 7372800 | tf_op jit(solution)/shard_map/pallas_call | solution.py:274
  160.7 5.3 %collective-permute-done.12 = bf16[2880,128]{1,0:T(8,128)(2,1)} collective-permute-done((bf16[2880,128]{1,0:T(8,128)(2,1)}, bf16[2880,128]{1,0:T(8,128)(2,1)}, u32[]{:S(2)}, u32[]{:S(2)}) %collective-permute-start.12) | collective-permute-done | bytes 737312 | tf_op jit(solution)/shard_map/ppermute | solution.py:310
  166.0 2.1 add_convert_fusion
  175.8 6.7 %shard_map.140 = f32[2880,128]{1,0:T(8,128)S(1)} custom-call(s32[10]{0:T(128)S(1)} %add_add_fusion.3.place_ref, f32[16]{0:T(128)S(1)} %dynamic_slice.24.sinks_ref, bf16[4,128,1024]{2,1,0:T(8,128)(2,1)S(1)} %copy-done.2, bf16[4,128,256]{2,1,0:T(8,128)(2,1)S(1)} %copy-done.4, bf16[4,128,256]{2,1,0:T(8,128)(2,1)S(1)} %copy-done.7, ...), custom_call_target="tpu_custom_call" | custom-call | flops 1023410176 | bytes 7372800 | tf_op jit(solution)/shard_map/pallas_call | solution.py:274
  182.5 2.8 collective-permute-done.13
  189.9 6.8 %all-to-all-start = ((bf16[32,8,2880]{2,1,0:T(8,128)(2,1)}), bf16[32,8,2880]{2,1,0:T(8,128)(2,1)}, u32[]{:S(2)}, u32[]{:S(2)}) async-start(bf16[32,8,2880]{2,1,0:T(8,128)(2,1)} %bitcast.25), calls=%async_computation | async-start | bytes 3014656 | tf_op jit(solution)/shard_map/all_to_all | solution.py:497
  197.5 2.2 reshape.201
  199.6 33.4 %all-to-all-done = bf16[32,8,2880]{2,1,0:T(8,128)(2,1)} async-done(((bf16[32,8,2880]{2,1,0:T(8,128)(2,1)}), bf16[32,8,2880]{2,1,0:T(8,128)(2,1)}, u32[]{:S(2)}, u32[]{:S(2)}) %all-to-all-start) | async-done | bytes 1474592 | tf_op jit(solution)/shard_map/all_to_all | solution.py:497
  233.1 14.6 %all-to-all-start.1 = ((bf16[32,3,4,2880]{3,2,1,0:T(4,128)(2,1)}), bf16[32,3,4,2880]{3,2,1,0:T(4,128)(2,1)S(1)}, u32[]{:S(2)}, u32[]{:S(2)}) async-start(bf16[32,3,4,2880]{3,2,1,0:T(4,128)(2,1)} %reshape.201), calls=%async_computation.1 | async-start | bytes 4521984 | tf_op jit(solution)/shard_map/all_to_all | solution.py:497
  247.6 23.5 %shard_map.143 = bf16[256,2880]{1,0:T(8,128)(2,1)} custom-call(bf16[256,2880]{1,0:T(8,128)(2,1)} %bitcast.26.rows_ref, bf16[2,2880,2880]{2,1,0:T(8,128)(2,1)} %bitcast.84, bf16[2,2880,2880]{2,1,0:T(8,128)(2,1)} %bitcast.85, bf16[2880,2880]{1,0:T(8,128)(2,1)} %bitcast.88), custom_call_target="tpu_custom_call" | custom-call | flops 12740198400 | bytes 52715520 | tf_op jit(solution)/shard_map/pallas_call | solution.py:420
  271.1 29.0 %all-to-all-done.1 = bf16[32,3,4,2880]{3,2,1,0:T(4,128)(2,1)S(1)} async-done(((bf16[32,3,4,2880]{3,2,1,0:T(4,128)(2,1)}), bf16[32,3,4,2880]{3,2,1,0:T(4,128)(2,1)S(1)}, u32[]{:S(2)}, u32[]{:S(2)}) %all-to-all-start.1) | async-done | bytes 2211872 | tf_op jit(solution)/shard_map/all_to_all | solution.py:497
  301.5 3.9 all-to-all-start.2
  305.4 4.3 %reshape.204.rows_ref = bf16[384,2880]{1,0:T(8,128)(2,1)} reshape(bf16[32,3,4,2880]{3,2,1,0:T(4,128)(2,1)} %copy-done.11) | data formatting | bytes 4423680 | tf_op jit(solution)/shard_map/reshape | solution.py:516
  309.7 29.2 %shard_map.144 = bf16[384,2880]{1,0:T(8,128)(2,1)} custom-call(bf16[384,2880]{1,0:T(8,128)(2,1)} %reshape.204.rows_ref, bf16[2,2880,2880]{2,1,0:T(8,128)(2,1)} %bitcast.86, bf16[2,2880,2880]{2,1,0:T(8,128)(2,1)} %bitcast.87, bf16[2880,2880]{1,0:T(8,128)(2,1)} %bitcast.89), custom_call_target="tpu_custom_call" | custom-call | flops 19110297600 | bytes 54190080 | tf_op jit(solution)/shard_map/pallas_call | solution.py:420
  338.9 4.1 reshape.205
  344.2 5.9 %all-to-all-start.3 = ((bf16[32,3,4,2880]{3,2,1,0:T(4,128)(2,1)}), bf16[32,3,4,2880]{3,2,1,0:T(4,128)(2,1)}, u32[]{:S(2)}, u32[]{:S(2)}) async-start(bf16[32,3,4,2880]{3,2,1,0:T(4,128)(2,1)} %reshape.205), calls=%async_computation.3 | async-start | bytes 4521984 | tf_op jit(solution)/shard_map/all_to_all | solution.py:497
  352.4 50.2 %all-to-all-done.3 = bf16[32,3,4,2880]{3,2,1,0:T(4,128)(2,1)} async-done(((bf16[32,3,4,2880]{3,2,1,0:T(4,128)(2,1)}), bf16[32,3,4,2880]{3,2,1,0:T(4,128)(2,1)}, u32[]{:S(2)}, u32[]{:S(2)}) %all-to-all-start.3) | async-done | bytes 2211872 | tf_op jit(solution)/shard_map/all_to_all | solution.py:497
  402.5 4.3 %reshape.208 = bf16[384,2880]{1,0:T(8,128)(2,1)} reshape(bf16[32,3,4,2880]{3,2,1,0:T(4,128)(2,1)} %all-to-all-done.3) | data formatting | bytes 4423680 | tf_op jit(solution)/shard_map/reshape | solution.py:530
  406.9 2.7 fusion.14
  (145 shorter events, 47.2 us)
Async XLA Ops:
  6.5 94.7 %all-gather.3.cloned.1.call-start = ((), (), s32[]{:S(2)}) async-start(), calls=%async_computation.4 | async-start | bytes 8331264 | tf_op jit(solution)/shard_map/all_gather | solution.py:330
  10.8 6.4 %copy-start.19 = (bf16[2880,128]{1,0:T(8,128)(2,1)}, bf16[2880,128]{1,0:T(8,128)(2,1)S(1)}, u32[]{:S(2)}) copy-start(bf16[2880,128]{1,0:T(8,128)(2,1)S(1)} %fusion.8.refs_0_) | copy-start | bytes 2211844
  11.1 10.4 %collective-permute-start = (bf16[96,1024]{1,0:T(8,128)(2,1)S(1)}, bf16[96,1024]{1,0:T(8,128)(2,1)S(1)}, u32[]{:S(2)}, u32[]{:S(2)}) collective-permute-start(bf16[96,1024]{1,0:T(8,128)(2,1)S(1)} %get-tuple-element.51), channel_id=1, source_target_pairs={{0,24},{1,25},{2,26},{3,27},{4,28},{5,29},{6,30},{7,31},{8,0},{9,1... | collective-permute-start | bytes 589832 | tf_op jit(solution)/shard_map/ppermute | solution.py:304
  16.2 17.6 %collective-permute-start.2 = (bf16[96,1024]{1,0:T(8,128)(2,1)S(1)}, bf16[96,1024]{1,0:T(8,128)(2,1)S(1)}, u32[]{:S(2)}, u32[]{:S(2)}) collective-permute-start(bf16[96,1024]{1,0:T(8,128)(2,1)S(1)} %get-tuple-element.49), channel_id=1, source_target_pairs={{0,8},{1,9},{2,10},{3,11},{4,12},{5,13},{6,14},{7,15},{8,16},{9,17... | collective-permute-start | bytes 589832 | tf_op jit(solution)/shard_map/ppermute | solution.py:304
  16.2 17.6 %collective-permute-start.1 = (bf16[96,1024]{1,0:T(8,128)(2,1)S(1)}, bf16[96,1024]{1,0:T(8,128)(2,1)S(1)}, u32[]{:S(2)}, u32[]{:S(2)}) collective-permute-start(bf16[96,1024]{1,0:T(8,128)(2,1)S(1)} %get-tuple-element.50), channel_id=1, source_target_pairs={{0,16},{1,17},{2,18},{3,19},{4,20},{5,21},{6,22},{7,23},{8,24},{9,... | collective-permute-start | bytes 589832 | tf_op jit(solution)/shard_map/ppermute | solution.py:304
  17.2 31.6 %collective-permute-start.3 = (bf16[2880,128]{1,0:T(8,128)(2,1)S(1)}, bf16[2880,128]{1,0:T(8,128)(2,1)}, u32[]{:S(2)}, u32[]{:S(2)}) collective-permute-start(bf16[2880,128]{1,0:T(8,128)(2,1)S(1)} %fusion.8.refs_0_), channel_id=1, source_target_pairs={{0,8},{1,9},{2,10},{3,11},{4,12},{5,13},{6,14},{7,15},{8,24},{9,25... | collective-permute-start | bytes 2211848 | tf_op jit(solution)/shard_map/ppermute | solution.py:310
  48.8 18.7 %collective-permute-start.4 = (bf16[2880,128]{1,0:T(8,128)(2,1)}, bf16[2880,128]{1,0:T(8,128)(2,1)S(1)}, u32[]{:S(2)}, u32[]{:S(2)}) collective-permute-start(bf16[2880,128]{1,0:T(8,128)(2,1)} %collective-permute-done.3.refs_1_), channel_id=1, source_target_pairs={{0,8},{1,9},{2,10},{3,11},{4,12},{5,13},{6,14},{7,15},{8,24},{9,25... | collective-permute-start | bytes 2211848 | tf_op jit(solution)/shard_map/ppermute | solution.py:310
  48.8 29.9 %collective-permute-start.7 = (bf16[4,96,1024]{2,1,0:T(8,128)(2,1)S(1)}, bf16[4,96,1024]{2,1,0:T(8,128)(2,1)S(1)}, u32[]{:S(2)}, u32[]{:S(2)}) collective-permute-start(bf16[4,96,1024]{2,1,0:T(8,128)(2,1)S(1)} %constant_dynamic-slice_fusion), channel_id=1, source_target_pairs={{0,6},{1,7},{2,4},{3,5},{4,2},{5,3},{6,0},{7,1},{8,14},{9,15},{10,... | collective-permute-start | bytes 2359304 | tf_op jit(solution)/shard_map/ppermute | solution.py:317
  51.2 42.7 %collective-permute-start.6 = (bf16[4,96,1024]{2,1,0:T(8,128)(2,1)S(1)}, bf16[4,96,1024]{2,1,0:T(8,128)(2,1)S(1)}, u32[]{:S(2)}, u32[]{:S(2)}) collective-permute-start(bf16[4,96,1024]{2,1,0:T(8,128)(2,1)S(1)} %constant_dynamic-slice_fusion), channel_id=1, source_target_pairs={{0,4},{1,5},{2,6},{3,7},{4,0},{5,1},{6,2},{7,3},{8,12},{9,13},{10,... | collective-permute-start | bytes 2359304 | tf_op jit(solution)/shard_map/ppermute | solution.py:317
  51.7 42.3 %collective-permute-start.5 = (bf16[4,96,1024]{2,1,0:T(8,128)(2,1)S(1)}, bf16[4,96,1024]{2,1,0:T(8,128)(2,1)S(1)}, u32[]{:S(2)}, u32[]{:S(2)}) collective-permute-start(bf16[4,96,1024]{2,1,0:T(8,128)(2,1)S(1)} %constant_dynamic-slice_fusion), channel_id=1, source_target_pairs={{0,2},{1,3},{2,0},{3,1},{4,6},{5,7},{6,4},{7,5},{8,10},{9,11},{10,... | collective-permute-start | bytes 2359304 | tf_op jit(solution)/shard_map/ppermute | solution.py:317
  67.5 26.5 %copy-start.27 = (bf16[2880,128]{1,0:T(8,128)(2,1)}, bf16[2880,128]{1,0:T(8,128)(2,1)S(1)}, u32[]{:S(2)}) copy-start(bf16[2880,128]{1,0:T(8,128)(2,1)S(1)} %collective-permute-done.4.refs_2_) | copy-start | bytes 2211844
  67.5 26.5 %collective-permute-start.8 = (bf16[2880,128]{1,0:T(8,128)(2,1)S(1)}, bf16[2880,128]{1,0:T(8,128)(2,1)S(1)}, u32[]{:S(2)}, u32[]{:S(2)}) collective-permute-start(bf16[2880,128]{1,0:T(8,128)(2,1)S(1)} %collective-permute-done.4.refs_2_), channel_id=1, source_target_pairs={{0,8},{1,9},{2,10},{3,11},{4,12},{5,13},{6,14},{7,15},{8,24},{9,25... | collective-permute-start | bytes 2211848 | tf_op jit(solution)/shard_map/ppermute | solution.py:310
  95.3 21.8 %collective-permute-start.10 = (bf16[4,4,96,1024]{3,2,1,0:T(8,128)(2,1)S(1)}, bf16[4,4,96,1024]{3,2,1,0:T(8,128)(2,1)}, u32[]{:S(2)}, u32[]{:S(2)}) collective-permute-start(bf16[4,4,96,1024]{3,2,1,0:T(8,128)(2,1)S(1)} %pad_maximum_fusion.even_ref), channel_id=1, source_target_pairs={{0,1},{1,0},{2,3},{3,2},{4,5},{5,4},{6,7},{7,6},{8,9},{9,8},{10,11... | collective-permute-start | bytes 9437192 | tf_op jit(solution)/shard_map/ppermute | solution.py:317
  101.3 13.0 %copy-start.29 = (f32[64]{0:T(128)S(1)}, f32[64]{0:T(128)}, u32[]{:S(2)}) copy-start(f32[64]{0:T(128)} %param.22) | copy-start | bytes 772
  111.9 6.9 %collective-permute-start.9 = (bf16[4,128,256]{2,1,0:T(8,128)(2,1)}, bf16[4,128,256]{2,1,0:T(8,128)(2,1)S(1)}, u32[]{:S(2)}, u32[]{:S(2)}) collective-permute-start(bf16[4,128,256]{2,1,0:T(8,128)(2,1)} %get-tuple-element.30.key_values_ref), channel_id=1, source_target_pairs={{0,1},{1,2},{2,3},{3,4},{4,5},{5,6},{6,7},{7,0},{8,9},{9,10},{10,1... | collective-permute-start | bytes 786440 | tf_op jit(solution)/shard_map/ppermute | solution.py:314
  118.9 10.8 %copy-start.5 = (bf16[4,128,256]{2,1,0:T(8,128)(2,1)}, bf16[4,128,256]{2,1,0:T(8,128)(2,1)S(1)}, u32[]{:S(2)}) copy-start(bf16[4,128,256]{2,1,0:T(8,128)(2,1)S(1)} %collective-permute-done.9.halos_ref) | copy-start | bytes 786436
  127.8 19.0 %collective-permute-start.11 = (bf16[2880,128]{1,0:T(8,128)(2,1)S(1)}, bf16[2880,128]{1,0:T(8,128)(2,1)S(1)}, u32[]{:S(2)}, u32[]{:S(2)}) collective-permute-start(bf16[2880,128]{1,0:T(8,128)(2,1)S(1)} %convert_element_type.111), channel_id=1, source_target_pairs={{0,8},{1,9},{2,10},{3,11},{4,12},{5,13},{6,14},{7,15},{8,24},{9,25... | collective-permute-start | bytes 2211848 | tf_op jit(solution)/shard_map/ppermute | solution.py:310
  136.3 13.0 %copy-start.25 = (s32[128,4]{0,1:T(4,128)S(1)}, s32[128,4]{0,1:T(4,128)}, u32[]{:S(2)}) copy-start(s32[128,4]{0,1:T(4,128)} %param.15) | copy-start | bytes 6148
  136.3 15.6 %copy-start.4 = (bf16[4,128,256]{2,1,0:T(8,128)(2,1)S(1)}, bf16[4,128,256]{2,1,0:T(8,128)(2,1)}, u32[]{:S(2)}) copy-start(bf16[4,128,256]{2,1,0:T(8,128)(2,1)} %get-tuple-element.30.key_values_ref) | copy-start | bytes 786436
  147.9 18.1 %collective-permute-start.12 = (bf16[2880,128]{1,0:T(8,128)(2,1)}, bf16[2880,128]{1,0:T(8,128)(2,1)}, u32[]{:S(2)}, u32[]{:S(2)}) collective-permute-start(bf16[2880,128]{1,0:T(8,128)(2,1)} %add_convert_fusion.1), channel_id=1, source_target_pairs={{0,8},{1,9},{2,10},{3,11},{4,12},{5,13},{6,14},{7,15},{8,24},{9,25... | collective-permute-start | bytes 2211848 | tf_op jit(solution)/shard_map/ppermute | solution.py:310
  160.7 7.9 %copy-start.26 = (f32[128,4]{0,1:T(4,128)S(1)}, f32[128,4]{0,1:T(4,128)}, u32[]{:S(2)}) copy-start(f32[128,4]{0,1:T(4,128)} %param.16) | copy-start | bytes 6148
  168.1 17.2 %collective-permute-start.13 = (bf16[2880,128]{1,0:T(8,128)(2,1)}, bf16[2880,128]{1,0:T(8,128)(2,1)}, u32[]{:S(2)}, u32[]{:S(2)}) collective-permute-start(bf16[2880,128]{1,0:T(8,128)(2,1)} %add_convert_fusion), channel_id=1, source_target_pairs={{0,8},{1,9},{2,10},{3,11},{4,12},{5,13},{6,14},{7,15},{8,24},{9,25... | collective-permute-start | bytes 2211848 | tf_op jit(solution)/shard_map/ppermute | solution.py:310
  175.8 9.6 %copy-start.15 = (bf16[128,2880]{0,1:T(8,128)(2,1)S(1)}, bf16[128,2880]{0,1:T(8,128)(2,1)}, u32[]{:S(2)}) copy-start(bf16[128,2880]{0,1:T(8,128)(2,1)} %param.14) | copy-start | bytes 2211844
  182.5 5.3 %copy-start.24 = (f32[2880]{0:T(1024)S(1)}, f32[2880]{0:T(1024)}, u32[]{:S(2)}) copy-start(f32[2880]{0:T(1024)} %param.18) | copy-start | bytes 34564
  189.9 43.2 %all-to-all-start = ((bf16[32,8,2880]{2,1,0:T(8,128)(2,1)}), bf16[32,8,2880]{2,1,0:T(8,128)(2,1)}, u32[]{:S(2)}, u32[]{:S(2)}) async-start(bf16[32,8,2880]{2,1,0:T(8,128)(2,1)} %bitcast.25), calls=%async_computation | async-start | bytes 3014656 | tf_op jit(solution)/shard_map/all_to_all | solution.py:497
  233.1 67.0 %all-to-all-start.1 = ((bf16[32,3,4,2880]{3,2,1,0:T(4,128)(2,1)}), bf16[32,3,4,2880]{3,2,1,0:T(4,128)(2,1)S(1)}, u32[]{:S(2)}, u32[]{:S(2)}) async-start(bf16[32,3,4,2880]{3,2,1,0:T(4,128)(2,1)} %reshape.201), calls=%async_computation.1 | async-start | bytes 4521984 | tf_op jit(solution)/shard_map/all_to_all | solution.py:497
  301.5 41.5 %all-to-all-start.2 = ((bf16[32,8,2880]{2,1,0:T(8,128)(2,1)}), bf16[32,8,2880]{2,1,0:T(8,128)(2,1)S(1)}, u32[]{:S(2)}, u32[]{:S(2)}) async-start(bf16[32,8,2880]{2,1,0:T(8,128)(2,1)} %bitcast.29), calls=%async_computation.2 | async-start | bytes 3014656 | tf_op jit(solution)/shard_map/all_to_all | solution.py:497
  343.0 7.4 %copy-start.16 = (f32[384,128]{1,0:T(8,128)S(1)}, f32[384,128]{1,0:T(8,128)}, u32[]{:S(2)}) copy-start(f32[384,128]{1,0:T(8,128)} %reshape.209) | copy-start | bytes 589828
  343.0 7.4 %copy-start.21 = (pred[384,128]{1,0:T(8,128)(4,1)S(1)}, pred[384,128]{1,0:T(8,128)(4,1)}, u32[]{:S(2)}) copy-start(pred[384,128]{1,0:T(8,128)(4,1)} %copy-done.20) | copy-start | bytes 147460
  344.2 58.4 %all-to-all-start.3 = ((bf16[32,3,4,2880]{3,2,1,0:T(4,128)(2,1)}), bf16[32,3,4,2880]{3,2,1,0:T(4,128)(2,1)}, u32[]{:S(2)}, u32[]{:S(2)}) async-start(bf16[32,3,4,2880]{3,2,1,0:T(4,128)(2,1)} %reshape.205), calls=%async_computation.3 | async-start | bytes 4521984 | tf_op jit(solution)/shard_map/all_to_all | solution.py:497
  352.4 54.5 %copy-start.22 = (bf16[384,128]{1,0:T(8,128)(2,1)S(1)}, bf16[384,128]{1,0:T(8,128)(2,1)}, u32[]{:S(2)}) copy-start(bf16[384,128]{1,0:T(8,128)(2,1)} %get-tuple-element.43) | copy-start | bytes 294916
  406.9 2.7 copy-start.13
  (17 other events, 19.6 us)
Sparse Core Ops, SparseCore 0:
  9.2 77.6 all-gather.2
where the time goes:
time: 420 us; the launch traced here: 418 us
  waiting for transfers between devices  203 us (48%)
  Pallas kernels  92.3 us (22%)
  starting transfers between devices  47.5 us (11%)
  local copies, waits for them, and re-layouts  35.7 us (9%)
  other arithmetic  17.8 us (4%)
  between operations  16.8 us (4%)
  matrix products  4.77 us (1%)
    all_to_all x4, waiting for transfers between devices, exchange(): return lax.all_to_all(parts, 'ctx', split_axis=0, concat_axis=0, tiled=True)  113 us
    pallas_call x2, Pallas kernels, run_expert(): pl.pallas_call(functools.partial(expert_kernel, tile, hidden), grid=(-(-h...  52.6 us
    ppermute x6, waiting for transfers between devices, pass_on(): return lax.ppermute(block, 'ctx', route)  48.6 us
    all_to_all x4, starting transfers between devices, exchange(): return lax.all_to_all(parts, 'ctx', split_axis=0, concat_axis=0, tiled=True)  31.2 us
    pallas_call x4, Pallas kernels, attend_and_project(): pl.pallas_call(functools.partial(attend_kernel, r), in_specs=[smem, smem]...  26.6 us
    ppermute x4, waiting for transfers between devices, swap(): return lax.ppermute(block, 'ctx', [(i, i ^ bits) for i in range(n_ctx)])  26.5 us
    ppermute x3, waiting for transfers between devices, shift(): lax.ppermute(block, 'ctx', [(i, (i + steps * PLANE) % n_ctx) for i in ran...  13.2 us
    unnamed x66, local copies, waits for them, and re-layouts  12.2 us
  transfers between devices with their start and end apart: 19, of which 13 were waited for; matrix products, arithmetic and copies ran while one was open for 7% of the time, Pallas kernels for 20%

commit v1 on v0

--- a/solution.py
+++ b/solution.py
@@ -71,7 +71,9 @@
     return jnp.dot(a, b, preferred_element_type=F32)
 
 
-def project_whole(tokens, gain_attn, query_weight, key_weight, value_weight, attn_sinks, out_weight):
+def project_whole(
+    tokens, gain_attn, query_weight, key_weight, value_weight, attn_sinks, out_weight, early
+):
     tok_dev = tokens.shape[0]
     full_rows = lax.all_gather(tokens, "exp", axis=1, tiled=True)
     normed = rms_norm(full_rows, gain_attn)
@@ -99,7 +101,7 @@
     )
     head_terms = dot32(attended, lax.all_gather(out_weight, "ctx", axis=1, tiled=True))
     attn_proj = lax.psum(head_terms.astype(BF16), "exp").astype(F32)
-    return (full_rows.astype(F32) + attn_proj).astype(BF16).T
+    return (full_rows.astype(F32) + attn_proj).astype(BF16).T, early
 
 
 def dot_nt(a, b):
@@ -193,14 +195,13 @@
 
 
 def attend_kernel(
-    r, place_ref, sinks_ref, queries_ref, key_values_ref, halos_ref, even_ref, odd_ref, out_ref, att_ref, total_ref
+    numbers, place_ref, sinks_ref, queries_ref, key_values_ref, halos_ref, even_ref, odd_ref, out_ref, att_ref, total_ref
 ):
-    q_ref, own_ref, previous_ref = queries_ref.at[r], key_values_ref.at[r], halos_ref.at[place_ref[1]]
-    rows = q_ref.shape[0]
+    count, rows = queries_ref.shape[:2]
     pair = 2 * HD
-    kv_heads = own_ref.shape[1] // pair
+    kv_heads = key_values_ref.shape[2] // pair
     kv_cols = kv_heads * HD
-    pairs = q_ref.shape[1] // pair
+    pairs = queries_ref.shape[2] // pair
     lane = lax.broadcasted_iota(jnp.int32, (rows, pair), 1)
     low = lane < HD
 
@@ -222,74 +223,79 @@
             tables.append((keys, values))
         return tables
 
-    own, previous = side(own_ref), side(previous_ref)
     row = lax.broadcasted_iota(jnp.int32, (rows, rows), 0)
     col = lax.broadcasted_iota(jnp.int32, (rows, rows), 1)
     inside = col <= row
-    shown = jnp.logical_or(inside, place_ref[0] == 0)
     scale = HD**-0.5
-    for p in range(pairs):
-        head = p * kv_heads // pairs
-        chunk = q_ref[:, p * pair : (p + 1) * pair]
-        scores_own = dot_nt(chunk, own[head][0])
-        scores_previous = dot_nt(chunk, previous[head][0])
-        probs_own, probs_previous = [], []
-        for h in range(2):
-            at = h * rows
-            scores = jnp.where(
-                inside, scores_own[:, at : at + rows], scores_previous[:, at : at + rows]
-            ) * scale
-            scores = jnp.where(shown, scores, -1e30)
-            sink = sinks_ref[2 * p + h]
-            top = jnp.maximum(jnp.max(scores, axis=1, keepdims=True), sink)
-            weights = jnp.exp(scores - top)
-            total = jnp.sum(weights, axis=1, keepdims=True) + jnp.exp(sink - top)
-            probs = weights / total
-            probs_own.append(jnp.where(inside, probs, 0.0).astype(BF16))
-            probs_previous.append(jnp.where(inside, 0.0, probs).astype(BF16))
-        mixed = dot32(jnp.concatenate(probs_own, axis=1), own[head][1])
-        mixed = mixed + dot32(jnp.concatenate(probs_previous, axis=1), previous[head][1])
-        att_ref[:, p * pair : (p + 1) * pair] = mixed.astype(BF16)
+    for i, r in enumerate(numbers):
+        own, previous = side(key_values_ref.at[r]), side(halos_ref.at[place_ref[count + r]])
+        shown = jnp.logical_or(inside, place_ref[r] == 0)
+        for p in range(pairs):
+            head = p * kv_heads // pairs
+            chunk = queries_ref[r, :, p * pair : (p + 1) * pair]
+            scores_own = dot_nt(chunk, own[head][0])
+            scores_previous = dot_nt(chunk, previous[head][0])
+            probs_own, probs_previous = [], []
+            for h in range(2):
+                at = h * rows
+                scores = jnp.where(
+                    inside, scores_own[:, at : at + rows], scores_previous[:, at : at + rows]
+                ) * scale
+                scores = jnp.where(shown, scores, -1e30)
+                sink = sinks_ref[2 * p + h]
+                top = jnp.maximum(jnp.max(scores, axis=1, keepdims=True), sink)
+                weights = jnp.exp(scores - top)
+                total = jnp.sum(weights, axis=1, keepdims=True) + jnp.exp(sink - top)
+                probs = weights / total
+                probs_own.append(jnp.where(inside, probs, 0.0).astype(BF16))
+                probs_previous.append(jnp.where(inside, 0.0, probs).astype(BF16))
+            mixed = dot32(jnp.concatenate(probs_own, axis=1), own[head][1])
+            mixed = mixed + dot32(jnp.concatenate(probs_previous, axis=1), previous[head][1])
+            att_ref[i * rows : (i + 1) * rows, p * pair : (p + 1) * pair] = mixed.astype(BF16)
 
     half, groups, padded, depth = even_ref.shape
-    cols = out_ref.shape[0] // (2 * half * groups)
+    cols = out_ref.shape[1] // (2 * half * groups)
     attended = att_ref[...]
     for side_at, weight_ref in enumerate((even_ref, odd_ref)):
         for i in range(half):
             terms = dot_nt(weight_ref[i].reshape(groups * padded, depth), attended)
-            share = place_ref[2 + 2 * i + side_at]
+            share = place_ref[2 * count + 2 * i + side_at]
             for g in range(groups):
                 total_ref[g, share] = terms[g * padded : (g + 1) * padded]
     for g in range(groups):
         for p in range(2 * half):
             at = (g * 2 * half + p) * cols
-            out_ref[at : at + cols, :] = total_ref[g, p, :cols, :]
-
-
-def attend_and_project(r, place, sinks, queries, key_values, halos, even, odd, width):
+            for i in range(len(numbers)):
+                out_ref[i, at : at + cols, :] = total_ref[g, p, :cols, i * rows : (i + 1) * rows]
+
+
+def attend_and_project(numbers, place, sinks, queries, key_values, halos, even, odd, width):
     rows = queries.shape[1]
+    count = len(numbers)
     half, groups, padded, depth = even.shape
     vmem = pl.BlockSpec(memory_space=pltpu.VMEM)
     smem = pl.BlockSpec(memory_space=pltpu.SMEM)
     return pl.pallas_call(
-        functools.partial(attend_kernel, r),
+        functools.partial(attend_kernel, numbers),
         in_specs=[smem, smem] + [vmem] * 5,
         out_specs=vmem,
-        out_shape=jax.ShapeDtypeStruct((width, rows), F32),
+        out_shape=jax.ShapeDtypeStruct((count, width, rows), F32),
         scratch_shapes=[
-            pltpu.VMEM((rows, depth), BF16),
-            pltpu.VMEM((groups, 2 * half, padded, rows), F32),
+            pltpu.VMEM((count * rows, depth), BF16),
+            pltpu.VMEM((groups, 2 * half, padded, count * rows), F32),
         ],
         compiler_params=pltpu.CompilerParams(vmem_limit_bytes=40 * 2**20),
         cost_estimate=pl.CostEstimate(
-            flops=2 * rows * depth * (width + 8 * rows),
-            bytes_accessed=2 * (width * depth + 2 * width * rows),
-            transcendentals=rows * rows * depth // HD,
+            flops=2 * count * rows * depth * (width + 8 * rows),
+            bytes_accessed=2 * width * (depth + 2 * count * rows),
+            transcendentals=count * rows * rows * depth // HD,
         ),
     )(place, sinks, queries, key_values, halos, even, odd)
 
 
-def project_planes(tokens, gain_attn, query_weight, key_weight, value_weight, attn_sinks, out_weight):
+def project_planes(
+    tokens, gain_attn, query_weight, key_weight, value_weight, attn_sinks, out_weight, early
+):
     tok_dev, width = tokens.shape
     n_ctx = lax.axis_size("ctx")
     n_z = n_ctx // PLANE
@@ -343,14 +349,6 @@
     ]
     ordered = jnp.stack(pieces[::-1] + pieces[:0:-1])
     out_mine = lax.dynamic_slice_in_dim(ordered, n_z - 1 - z, n_z, 0)
-    out_mine, blocks[1] = lax.optimization_barrier((out_mine, blocks[1]))
-    for _ in range(n_z - 2):
-        blocks.append(pass_on(blocks[-1]))
-    out_parts = [out_mine] + [swap(out_mine, bits) for bits in (2, 4, 6)]
-    out_parts, blocks[-1] = lax.optimization_barrier((out_parts, blocks[-1]))
-    out_half = jnp.stack(out_parts)
-    out_other = swap(out_half, 1)
-
     heads = PLANE * query_weight.shape[1] // HD
     sinks = lax.dynamic_slice_in_dim(attn_sinks, z * heads, heads)
     own_rows = jnp.arange(tok_dev, dtype=jnp.int32)
@@ -362,27 +360,34 @@
     numbers = block_z * PLANE + j
     angles = (numbers[:, None] * tok_dev + own_rows[None, :]).astype(F32)[:, :, None] * inverse_freq
     signed_sine = jnp.where(lane < half, -jnp.sin(angles), jnp.sin(angles))
-    queries, key_values = project_blocks(blocks, weights, share, jnp.cos(angles), signed_sine)
-    halos = behind(key_values)
+    cosine = jnp.cos(angles)
     below = (places[jnp.maximum(block_z - 1, 0)] - mine) % n_z
     previous_at = jnp.where(j == 0, below, jnp.arange(n_z, dtype=jnp.int32))
-
     relative = jnp.arange(PLANE, dtype=jnp.int32) ^ j
-    partial_sums = []
-    for r in list(range(1, n_z)) + [0]:
-        first = (numbers[r] == 0).astype(jnp.int32)
-        place = jnp.concatenate([jnp.stack([first, previous_at[r]]), relative])
-        partial_sums.append(
-            attend_and_project(
-                r, place, sinks, queries, key_values, halos, out_half, out_other, width
-            )
+    place = jnp.concatenate([(numbers == 0).astype(jnp.int32), previous_at, relative])
+    (out_mine, blocks[1], cosine, signed_sine, place, sinks, early) = lax.optimization_barrier(
+        (out_mine, blocks[1], cosine, signed_sine, place, sinks, early)
+    )
+    for _ in range(n_z - 2):
+        blocks.append(pass_on(blocks[-1]))
+    out_parts = [out_mine] + [swap(out_mine, bits) for bits in (2, 4, 6)]
+    out_parts, blocks[-1] = lax.optimization_barrier((out_parts, blocks[-1]))
+    out_half = jnp.stack(out_parts)
+    out_other = swap(out_half, 1)
+    queries, key_values = project_blocks(blocks, weights, share, cosine, signed_sine)
+    halos = behind(key_values)
+
+    def parts_of(numbers):
+        return attend_and_project(
+            numbers, place, sinks, queries, key_values, halos, out_half, out_other, width
         )
-    running = partial_sums[0].astype(BF16)
-    for term in partial_sums[1:]:
-        running = pass_on(running).astype(F32) + term
-        if term is not partial_sums[-1]:
-            running = running.astype(BF16)
-    return (tokens_t.astype(F32) + running).astype(BF16)
+
+    running = parts_of((1,))[0].astype(BF16)
+    others = parts_of(tuple(range(2, n_z)) + (0,))
+    for i in range(n_z - 2):
+        running = (pass_on(running).astype(F32) + others[i]).astype(BF16)
+    total = pass_on(running).astype(F32) + others[n_z - 2]
+    return (tokens_t.astype(F32) + total).astype(BF16), early
 
 
 def expert_kernel(tile, hidden, rows_ref, gate_ref, upper_ref, down_ref, out_ref, total_ref):
@@ -439,8 +444,7 @@
 
 
 def slot_chunks(capacity):
-    first = min(8, capacity)
-    return [first, capacity - first] if capacity > first else [first]
+    return [min(8, capacity - first) for first in range(0, capacity, 8)]
 
 
 def dispatch_kernel(chosen_ref, normed_ref, out_ref):
@@ -460,7 +464,7 @@
     )(chosen, normed)
 
 
-def routing(route_ids, combine, n_ctx, capacity):
+def routing(route_ids, combine, n_ctx, sizes):
     tok_dev = route_ids.shape[0]
     named = route_ids[:, :, None] == jnp.arange(n_ctx, dtype=jnp.int32)[None, None, :]
     member = jnp.any(named, axis=1)
@@ -472,18 +476,18 @@
     weight_of = weight_of.T
     chunks = []
     first = 0
-    for size in slot_chunks(capacity):
+    for size in sizes:
         slots = first + jnp.arange(size, dtype=jnp.int32)
         chosen = (slot_of[:, None, :] == slots[None, :, None]).reshape(n_ctx * size, tok_dev)
         scale = jnp.where(chosen, jnp.repeat(weight_of, size, axis=0), 0.0)
         high = scale.astype(BF16)
         low = (scale - high.astype(F32)).astype(BF16)
-        chunks.append((size, chosen.astype(BF16), jnp.concatenate([high, low], axis=1)))
+        chunks.append((chosen.astype(BF16), jnp.concatenate([high, low], axis=1)))
         first += size
     return chunks
 
 
-def mix_experts(normed, chunks, gate_up, down):
+def mix_experts(normed, sizes, matrices, gate_up, down):
     width, tok_dev = normed.shape
     n_ctx, n_exp = lax.axis_size("ctx"), lax.axis_size("exp")
     width_local = width // n_exp
@@ -500,7 +504,7 @@
         return lax.optimization_barrier((parts, earlier))
 
     outgoing, received = [], []
-    for size, chosen, _ in chunks:
+    for size, (chosen, _) in zip(sizes, matrices):
         if outgoing:
             chosen, outgoing[-1] = in_order(chosen, outgoing[-1])
         outgoing.append(tiles(dispatch(chosen, normed), size))
@@ -510,7 +514,9 @@
         received.append(exchange(parts))
 
     results = []
-    for i, (size, _, _) in enumerate(chunks):
+    for i, size in enumerate(sizes):
+        if i > 1 and i == len(sizes) - 1:
+            received[i], results[0] = in_order(received[i], results[0])
         if results:
             received[i], results[-1] = in_order(received[i], results[-1])
         rows_in = received[i].reshape(n_ctx * size, width)
@@ -523,7 +529,7 @@
         answers.append(exchange(parts))
 
     moe_out = jnp.zeros((width_local, tok_dev), F32)
-    for (size, _, scale), answer in zip(chunks, answers):
+    for size, (_, scale), answer in zip(sizes, matrices, answers):
         if n_exp > 1:
             answer = lax.psum_scatter(answer, "exp", scatter_dimension=answer.ndim - 1, tiled=True)
         terms = lax.dot_general(
@@ -552,18 +558,19 @@
     n_ctx = lax.axis_size("ctx")
     n_exp = lax.axis_size("exp")
     capacity = tok_dev * route_ids.shape[1] * 5 // (4 * n_ctx)
-    chunks = routing(route_ids, combine, n_ctx, capacity)
+    sizes = slot_chunks(capacity)
+    matrices = routing(route_ids, combine, n_ctx, sizes)
     by_planes = n_exp == 1 and n_ctx % PLANE == 0 and n_ctx > PLANE
     project = project_planes if by_planes else project_whole
-    residual = project(
-        tokens, gain_attn, query_weight, key_weight, value_weight, attn_sinks, out_weight
+    residual, matrices = project(
+        tokens, gain_attn, query_weight, key_weight, value_weight, attn_sinks, out_weight, matrices
     )
     width = residual.shape[0]
     normed_moe = rms_norm_t(residual, gain_moe)
     exp_index = lax.axis_index("exp")
     residual_local = lax.dynamic_slice_in_dim(residual, exp_index * width_local, width_local, 0)
 
-    moe_out = mix_experts(normed_moe, chunks, gate_up_weight[0], down_weight[0])
+    moe_out = mix_experts(normed_moe, sizes, matrices, gate_up_weight[0], down_weight[0])
     return (residual_local.astype(F32) + moe_out).astype(BF16).T
 
 

time: 420 us -> 417 us (level); the launches traced: 418 us -> 409 us
  local copies, waits for them, and re-layouts: 35.7 us -> 16.7 us
  waiting for transfers between devices: 203 us -> 219 us
  other arithmetic: 17.8 us -> 10.4 us
  Pallas kernels: 92.3 us -> 99.6 us
  starting transfers between devices: 47.5 us -> 42.9 us
    ppermute x6, waiting for transfers between devices: 48.6 us -> 69.3 us  [pass_on(): return lax.ppermute(block, 'ctx', route)]
    pallas_call x2 -> x3, Pallas kernels: 52.6 us -> 64.5 us  [run_expert(): pl.pallas_call(functools.partial(expert_kernel, tile, hidden), grid=(-(-h...]
    ppermute x3, waiting for transfers between devices: 13.2 us -> 3.87 us  [shift(): lax.ppermute(block, 'ctx', [(i, (i + steps * PLANE) % n_ctx) for i in ran...]
    pallas_call x4 -> x2, Pallas kernels: 26.6 us -> 20.6 us  [attend_and_project(): pl.pallas_call(functools.partial(attend_kernel, numbers), in_specs=[smem,...]
    ppermute x1, waiting for transfers between devices: 1.8 us -> 6.46 us  [behind(): return lax.ppermute(block, 'ctx', route)]
    unnamed x66 -> x54, local copies, waits for them, and re-layouts: 12.2 us -> 8.03 us
    all_to_all x4 -> x6, starting transfers between devices: 31.2 us -> 28.3 us  [exchange(): return lax.all_to_all(parts, 'ctx', split_axis=0, concat_axis=0, tiled=True)]
    all_to_all x4 -> x6, waiting for transfers between devices: 113 us -> 114 us  [exchange(): return lax.all_to_all(parts, 'ctx', split_axis=0, concat_axis=0, tiled=True)]
  transfers between devices with their start and end apart: 19 -> 21, of which waited for: 13 -> 15; matrix products, arithmetic and copies ran while one was open for 7% -> 4% of each run, Pallas kernels for 20% -> 22%
where the time goes in v1:
time: 417 us; the launch traced here: 409 us
  waiting for transfers between devices  219 us (53%)
  Pallas kernels  99.6 us (24%)
  starting transfers between devices  42.9 us (10%)
  local copies, waits for them, and re-layouts  16.7 us (4%)
  between operations  14.6 us (4%)
  other arithmetic  10.4 us (2%)
  matrix products  6.21 us (1%)
    all_to_all x6, waiting for transfers between devices, exchange(): return lax.all_to_all(parts, 'ctx', split_axis=0, concat_axis=0, tiled=True)  114 us
    ppermute x6, waiting for transfers between devices, pass_on(): return lax.ppermute(block, 'ctx', route)  69.3 us
    pallas_call x3, Pallas kernels, run_expert(): pl.pallas_call(functools.partial(expert_kernel, tile, hidden), grid=(-(-h...  64.5 us
    all_to_all x6, starting transfers between devices, exchange(): return lax.all_to_all(parts, 'ctx', split_axis=0, concat_axis=0, tiled=True)  28.3 us
    ppermute x4, waiting for transfers between devices, swap(): return lax.ppermute(block, 'ctx', [(i, i ^ bits) for i in range(n_ctx)])  24.8 us
    pallas_call x2, Pallas kernels, attend_and_project(): pl.pallas_call(functools.partial(attend_kernel, numbers), in_specs=[smem,...  20.6 us
    pallas_call x1, Pallas kernels, project_blocks(): pl.pallas_call(functools.partial(qkv_kernel, count), grid=(PLANE // 2,),...  10.7 us
  transfers between devices with their start and end apart: 21, of which 15 were waited for; matrix products, arithmetic and copies ran while one was open for 4% of the time, Pallas kernels for 22%

profile of v1, /device:TPU:0, one launch (start us, length us, event | category | flops | bytes accessed | tf_op | source)
XLA Modules:
  0.0 409.0 jit_solution(6638241992043754749)
XLA Ops:
  11.1 3.1 collective-permute-start.2
  14.2 2.6 collective-permute-start.1
  25.8 2.2 collective-permute-done
  29.9 19.8 %collective-permute-done.3.refs_1_ = bf16[2880,128]{1,0:T(8,128)(2,1)} collective-permute-done((bf16[2880,128]{1,0:T(8,128)(2,1)S(1)}, bf16[2880,128]{1,0:T(8,128)(2,1)}, u32[]{:S(2)}, u32[]{:S(2)}) %collective-permute-start.3) | collective-permute-done | bytes 737312 | tf_op jit(solution)/shard_map/ppermute | solution.py:316
  49.7 2.4 collective-permute-start.7
  53.2 16.0 %collective-permute-done.4.refs_2_ = bf16[2880,128]{1,0:T(8,128)(2,1)S(1)} collective-permute-done((bf16[2880,128]{1,0:T(8,128)(2,1)}, bf16[2880,128]{1,0:T(8,128)(2,1)S(1)}, u32[]{:S(2)}, u32[]{:S(2)}) %collective-permute-start.4) | collective-permute-done | bytes 737312 | tf_op jit(solution)/shard_map/ppermute | solution.py:316
  69.2 9.1 %collective-permute-done.7 = bf16[4,96,1024]{2,1,0:T(8,128)(2,1)S(1)} collective-permute-done((bf16[4,96,1024]{2,1,0:T(8,128)(2,1)S(1)}, bf16[4,96,1024]{2,1,0:T(8,128)(2,1)S(1)}, u32[]{:S(2)}, u32[]{:S(2)}) %collective-permute-start.7) | collective-permute-done | bytes 786464 | tf_op jit(solution)/shard_map/ppermute | solution.py:323
  78.4 15.6 %collective-permute-done.6 = bf16[4,96,1024]{2,1,0:T(8,128)(2,1)S(1)} collective-permute-done((bf16[4,96,1024]{2,1,0:T(8,128)(2,1)S(1)}, bf16[4,96,1024]{2,1,0:T(8,128)(2,1)S(1)}, u32[]{:S(2)}, u32[]{:S(2)}) %collective-permute-start.6) | collective-permute-done | bytes 786464 | tf_op jit(solution)/shard_map/ppermute | solution.py:323
  95.4 10.7 %shard_map.136 = (bf16[4,128,1024]{2,1,0:T(8,128)(2,1)}, bf16[4,128,256]{2,1,0:T(8,128)(2,1)}) custom-call(bf16[2880,128]{1,0:T(8,128)(2,1)} %copy-done.15, bf16[2880,128]{1,0:T(8,128)(2,1)} %collective-permute-done.3.refs_1_, bf16[2880,128]{1,0:T(8,128)(2,1)} %copy-done.21, bf16[2880,128]{1,0:T(8,128)(2,1)} %copy-done.22, bf16[8,3616,128]{2,1,0:T(8,128)(2,1)} %bitcast.165, ...), custom_call_target="tpu_custom_call" | custom-call | flops 3774873600 | bytes 10321920 | tf_op jit(solution)/shard_map/pallas_call | solution.py:167
  106.5 6.5 %collective-permute-done.9.halos_ref = bf16[4,128,256]{2,1,0:T(8,128)(2,1)S(1)} collective-permute-done((bf16[4,128,256]{2,1,0:T(8,128)(2,1)}, bf16[4,128,256]{2,1,0:T(8,128)(2,1)S(1)}, u32[]{:S(2)}, u32[]{:S(2)}) %collective-permute-start.9) | collective-permute-done | bytes 262176 | tf_op jit(solution)/shard_map/ppermute | solution.py:320
  115.2 6.6 %shard_map.137 = f32[1,2880,128]{2,1,0:T(8,128)S(1)} custom-call(s32[16]{0:T(128)S(1)} %pad_add_fusion.place_ref, f32[16]{0:T(128)S(1)} %dynamic_slice.29.sinks_ref, bf16[4,128,1024]{2,1,0:T(8,128)(2,1)S(1)} %copy-done, bf16[4,128,256]{2,1,0:T(8,128)(2,1)S(1)} %copy-done.1, bf16[4,128,256]{2,1,0:T(8,128)(2,1)S(1)} %collective-permute-done.9.halos_ref, ...), custom_call_target="tpu_custom_call" | custom-call | flops 1023410176 | bytes 7372800 | tf_op jit(solution)/shard_map/pallas_call | solution.py:278
  123.6 14.0 %shard_map.138 = f32[3,2880,128]{2,1,0:T(8,128)S(1)} custom-call(s32[16]{0:T(128)S(1)} %pad_add_fusion.place_ref, f32[16]{0:T(128)S(1)} %dynamic_slice.29.sinks_ref, bf16[4,128,1024]{2,1,0:T(8,128)(2,1)S(1)} %copy-done, bf16[4,128,256]{2,1,0:T(8,128)(2,1)S(1)} %copy-done.1, bf16[4,128,256]{2,1,0:T(8,128)(2,1)S(1)} %collective-permute-done.9.halos_ref, ...), custom_call_target="tpu_custom_call" | custom-call | flops 3070230528 | bytes 10321920 | tf_op jit(solution)/shard_map/pallas_call | solution.py:278
  137.6 2.1 collective-permute-done.11
  140.5 16.1 %collective-permute-done.12 = bf16[2880,128]{1,0:T(8,128)(2,1)S(1)} collective-permute-done((bf16[2880,128]{1,0:T(8,128)(2,1)S(1)}, bf16[2880,128]{1,0:T(8,128)(2,1)S(1)}, u32[]{:S(2)}, u32[]{:S(2)}) %collective-permute-start.12) | collective-permute-done | bytes 737312 | tf_op jit(solution)/shard_map/ppermute | solution.py:316
  157.3 15.3 %collective-permute-done.13 = bf16[2880,128]{1,0:T(8,128)(2,1)S(1)} collective-permute-done((bf16[2880,128]{1,0:T(8,128)(2,1)S(1)}, bf16[2880,128]{1,0:T(8,128)(2,1)S(1)}, u32[]{:S(2)}, u32[]{:S(2)}) %collective-permute-start.13) | collective-permute-done | bytes 737312 | tf_op jit(solution)/shard_map/ppermute | solution.py:316
  175.2 6.5 %all-to-all-start = ((bf16[32,8,2880]{2,1,0:T(8,128)(2,1)}), bf16[32,8,2880]{2,1,0:T(8,128)(2,1)S(1)}, u32[]{:S(2)}, u32[]{:S(2)}) async-start(bf16[32,8,2880]{2,1,0:T(8,128)(2,1)} %bitcast.33), calls=%async_computation | async-start | bytes 3014656 | tf_op jit(solution)/shard_map/all_to_all | solution.py:501
  183.3 34.7 %all-to-all-done = bf16[32,8,2880]{2,1,0:T(8,128)(2,1)S(1)} async-done(((bf16[32,8,2880]{2,1,0:T(8,128)(2,1)}), bf16[32,8,2880]{2,1,0:T(8,128)(2,1)S(1)}, u32[]{:S(2)}, u32[]{:S(2)}) %all-to-all-start) | async-done | bytes 1474592 | tf_op jit(solution)/shard_map/all_to_all | solution.py:501
  219.2 3.8 all-to-all-start.1
  224.4 34.9 %all-to-all-done.1 = bf16[32,8,2880]{2,1,0:T(8,128)(2,1)} async-done(((bf16[32,8,2880]{2,1,0:T(8,128)(2,1)}), bf16[32,8,2880]{2,1,0:T(8,128)(2,1)}, u32[]{:S(2)}, u32[]{:S(2)}) %all-to-all-start.1) | async-done | bytes 1474592 | tf_op jit(solution)/shard_map/all_to_all | solution.py:501
  259.4 4.0 all-to-all-start.2
  263.4 23.4 %shard_map.142 = bf16[256,2880]{1,0:T(8,128)(2,1)} custom-call(bf16[256,2880]{1,0:T(8,128)(2,1)} %bitcast.149, bf16[2,2880,2880]{2,1,0:T(8,128)(2,1)} %bitcast.140, bf16[2,2880,2880]{2,1,0:T(8,128)(2,1)} %bitcast.141, bf16[2880,2880]{1,0:T(8,128)(2,1)} %bitcast.146), custom_call_target="tpu_custom_call" | custom-call | flops 12740198400 | bytes 52715520 | tf_op jit(solution)/shard_map/pallas_call | solution.py:425
  286.8 6.2 %all-to-all-start.3 = ((bf16[32,8,2880]{2,1,0:T(8,128)(2,1)}), bf16[32,8,2880]{2,1,0:T(8,128)(2,1)S(1)}, u32[]{:S(2)}, u32[]{:S(2)}) async-start(bf16[32,8,2880]{2,1,0:T(8,128)(2,1)} %bitcast.39), calls=%async_computation.3 | async-start | bytes 3014656 | tf_op jit(solution)/shard_map/all_to_all | solution.py:501
  293.0 23.5 %shard_map.143 = bf16[256,2880]{1,0:T(8,128)(2,1)} custom-call(bf16[256,2880]{1,0:T(8,128)(2,1)} %bitcast.40.rows_ref, bf16[2,2880,2880]{2,1,0:T(8,128)(2,1)} %bitcast.142, bf16[2,2880,2880]{2,1,0:T(8,128)(2,1)} %bitcast.143, bf16[2880,2880]{1,0:T(8,128)(2,1)} %bitcast.147), custom_call_target="tpu_custom_call" | custom-call | flops 12740198400 | bytes 52715520 | tf_op jit(solution)/shard_map/pallas_call | solution.py:425
  316.5 12.9 %all-to-all-done.3 = bf16[32,8,2880]{2,1,0:T(8,128)(2,1)S(1)} async-done(((bf16[32,8,2880]{2,1,0:T(8,128)(2,1)}), bf16[32,8,2880]{2,1,0:T(8,128)(2,1)S(1)}, u32[]{:S(2)}, u32[]{:S(2)}) %all-to-all-start.3) | async-done | bytes 1474592 | tf_op jit(solution)/shard_map/all_to_all | solution.py:501
  330.5 3.7 all-to-all-start.4
  335.8 17.7 %shard_map.144 = bf16[128,2880]{1,0:T(8,128)(2,1)S(1)} custom-call(bf16[128,2880]{1,0:T(8,128)(2,1)S(1)} %reshape.215.rows_ref, bf16[2,2880,2880]{2,1,0:T(8,128)(2,1)} %bitcast.144, bf16[2,2880,2880]{2,1,0:T(8,128)(2,1)} %bitcast.145, bf16[2880,2880]{1,0:T(8,128)(2,1)} %bitcast.148), custom_call_target="tpu_custom_call" | custom-call | flops 6370099200 | bytes 51240960 | tf_op jit(solution)/shard_map/pallas_call | solution.py:425
  354.5 16.1 %all-to-all-done.4 = bf16[32,8,2880]{2,1,0:T(8,128)(2,1)S(1)} async-done(((bf16[32,8,2880]{2,1,0:T(8,128)(2,1)}), bf16[32,8,2880]{2,1,0:T(8,128)(2,1)S(1)}, u32[]{:S(2)}, u32[]{:S(2)}) %all-to-all-start.4) | async-done | bytes 1474592 | tf_op jit(solution)/shard_map/all_to_all | solution.py:501
  371.7 4.1 %all-to-all-start.5 = ((bf16[32,1,4,2880]{3,2,1,0:T(4,128)(2,1)}), bf16[32,1,4,2880]{3,2,1,0:T(4,128)(2,1)}, u32[]{:S(2)}, u32[]{:S(2)}) async-start(bf16[32,1,4,2880]{3,2,1,0:T(4,128)(2,1)} %bitcast.44), calls=%async_computation.5 | async-start | bytes 1507328 | tf_op jit(solution)/shard_map/all_to_all | solution.py:501
  375.9 2.1 fusion.2
  378.0 2.2 fusion
  380.1 15.6 %all-to-all-done.5 = bf16[32,1,4,2880]{3,2,1,0:T(4,128)(2,1)} async-done(((bf16[32,1,4,2880]{3,2,1,0:T(4,128)(2,1)}), bf16[32,1,4,2880]{3,2,1,0:T(4,128)(2,1)}, u32[]{:S(2)}, u32[]{:S(2)}) %all-to-all-start.5) | async-done | bytes 737312 | tf_op jit(solution)/shard_map/all_to_all | solution.py:501
  395.7 2.3 reshape.218
  (139 shorter events, 38.7 us)
Async XLA Ops:
  6.5 88.9 %all-gather.3.cloned.1.call-start = ((), (), s32[]{:S(2)}) async-start(), calls=%async_computation.6 | async-start | bytes 8331264 | tf_op jit(solution)/shard_map/all_gather | solution.py:336
  10.8 7.3 %copy-start.15 = (bf16[2880,128]{1,0:T(8,128)(2,1)}, bf16[2880,128]{1,0:T(8,128)(2,1)S(1)}, u32[]{:S(2)}) copy-start(bf16[2880,128]{1,0:T(8,128)(2,1)S(1)} %fusion.17.refs_0_) | copy-start | bytes 2211844
  10.9 7.9 %copy-start.2 = (s32[4]{0:T(128)S(1)}, s32[4]{0:T(128)}, u32[]{:S(2)}) copy-start(s32[4]{0:T(128)} %constant.147.clone) | copy-start | bytes 52
  10.9 9.1 %copy-start.3 = (s32[4]{0:T(128)S(1)}, s32[4]{0:T(128)}, u32[]{:S(2)}) copy-start(s32[4]{0:T(128)} %constant.146.clone) | copy-start | bytes 52
  11.0 10.6 %copy-start.19 = (s32[128,4]{0,1:T(4,128)S(1)}, s32[128,4]{0,1:T(4,128)}, u32[]{:S(2)}) copy-start(s32[128,4]{0,1:T(4,128)} %param.15) | copy-start | bytes 6148
  11.1 10.6 %copy-start.20 = (f32[128,4]{0,1:T(4,128)S(1)}, f32[128,4]{0,1:T(4,128)}, u32[]{:S(2)}) copy-start(f32[128,4]{0,1:T(4,128)} %param.16) | copy-start | bytes 6148
  11.1 10.9 %copy-start.23 = (f32[64]{0:T(128)S(1)}, f32[64]{0:T(128)}, u32[]{:S(2)}) copy-start(f32[64]{0:T(128)} %param.22) | copy-start | bytes 772
  11.1 18.6 %collective-permute-start.2 = (bf16[96,1024]{1,0:T(8,128)(2,1)S(1)}, bf16[96,1024]{1,0:T(8,128)(2,1)S(1)}, u32[]{:S(2)}, u32[]{:S(2)}) collective-permute-start(bf16[96,1024]{1,0:T(8,128)(2,1)S(1)} %get-tuple-element.87), channel_id=1, source_target_pairs={{0,8},{1,9},{2,10},{3,11},{4,12},{5,13},{6,14},{7,15},{8,16},{9,17... | collective-permute-start | bytes 589832 | tf_op jit(solution)/shard_map/ppermute | solution.py:310
  14.2 15.5 %collective-permute-start.1 = (bf16[96,1024]{1,0:T(8,128)(2,1)S(1)}, bf16[96,1024]{1,0:T(8,128)(2,1)S(1)}, u32[]{:S(2)}, u32[]{:S(2)}) collective-permute-start(bf16[96,1024]{1,0:T(8,128)(2,1)S(1)} %get-tuple-element.88), channel_id=1, source_target_pairs={{0,16},{1,17},{2,18},{3,19},{4,20},{5,21},{6,22},{7,23},{8,24},{9,... | collective-permute-start | bytes 589832 | tf_op jit(solution)/shard_map/ppermute | solution.py:310
  16.8 11.2 %collective-permute-start = (bf16[96,1024]{1,0:T(8,128)(2,1)S(1)}, bf16[96,1024]{1,0:T(8,128)(2,1)S(1)}, u32[]{:S(2)}, u32[]{:S(2)}) collective-permute-start(bf16[96,1024]{1,0:T(8,128)(2,1)S(1)} %get-tuple-element.89), channel_id=1, source_target_pairs={{0,24},{1,25},{2,26},{3,27},{4,28},{5,29},{6,30},{7,31},{8,0},{9,1... | collective-permute-start | bytes 589832 | tf_op jit(solution)/shard_map/ppermute | solution.py:310
  18.2 31.6 %collective-permute-start.3 = (bf16[2880,128]{1,0:T(8,128)(2,1)S(1)}, bf16[2880,128]{1,0:T(8,128)(2,1)}, u32[]{:S(2)}, u32[]{:S(2)}) collective-permute-start(bf16[2880,128]{1,0:T(8,128)(2,1)S(1)} %fusion.17.refs_0_), channel_id=1, source_target_pairs={{0,8},{1,9},{2,10},{3,11},{4,12},{5,13},{6,14},{7,15},{8,24},{9,25... | collective-permute-start | bytes 2211848 | tf_op jit(solution)/shard_map/ppermute | solution.py:316
  49.7 19.5 %collective-permute-start.4 = (bf16[2880,128]{1,0:T(8,128)(2,1)}, bf16[2880,128]{1,0:T(8,128)(2,1)S(1)}, u32[]{:S(2)}, u32[]{:S(2)}) collective-permute-start(bf16[2880,128]{1,0:T(8,128)(2,1)} %collective-permute-done.3.refs_1_), channel_id=1, source_target_pairs={{0,8},{1,9},{2,10},{3,11},{4,12},{5,13},{6,14},{7,15},{8,24},{9,25... | collective-permute-start | bytes 2211848 | tf_op jit(solution)/shard_map/ppermute | solution.py:316
  49.7 28.7 %collective-permute-start.7 = (bf16[4,96,1024]{2,1,0:T(8,128)(2,1)S(1)}, bf16[4,96,1024]{2,1,0:T(8,128)(2,1)S(1)}, u32[]{:S(2)}, u32[]{:S(2)}) collective-permute-start(bf16[4,96,1024]{2,1,0:T(8,128)(2,1)S(1)} %constant_dynamic-slice_fusion), channel_id=1, source_target_pairs={{0,6},{1,7},{2,4},{3,5},{4,2},{5,3},{6,0},{7,1},{8,14},{9,15},{10,... | collective-permute-start | bytes 2359304 | tf_op jit(solution)/shard_map/ppermute | solution.py:323
  52.1 41.8 %collective-permute-start.6 = (bf16[4,96,1024]{2,1,0:T(8,128)(2,1)S(1)}, bf16[4,96,1024]{2,1,0:T(8,128)(2,1)S(1)}, u32[]{:S(2)}, u32[]{:S(2)}) collective-permute-start(bf16[4,96,1024]{2,1,0:T(8,128)(2,1)S(1)} %constant_dynamic-slice_fusion), channel_id=1, source_target_pairs={{0,4},{1,5},{2,6},{3,7},{4,0},{5,1},{6,2},{7,3},{8,12},{9,13},{10,... | collective-permute-start | bytes 2359304 | tf_op jit(solution)/shard_map/ppermute | solution.py:323
  52.6 41.4 %collective-permute-start.5 = (bf16[4,96,1024]{2,1,0:T(8,128)(2,1)S(1)}, bf16[4,96,1024]{2,1,0:T(8,128)(2,1)S(1)}, u32[]{:S(2)}, u32[]{:S(2)}) collective-permute-start(bf16[4,96,1024]{2,1,0:T(8,128)(2,1)S(1)} %constant_dynamic-slice_fusion), channel_id=1, source_target_pairs={{0,2},{1,3},{2,0},{3,1},{4,6},{5,7},{6,4},{7,5},{8,10},{9,11},{10,... | collective-permute-start | bytes 2359304 | tf_op jit(solution)/shard_map/ppermute | solution.py:323
  69.2 24.8 %copy-start.21 = (bf16[2880,128]{1,0:T(8,128)(2,1)}, bf16[2880,128]{1,0:T(8,128)(2,1)S(1)}, u32[]{:S(2)}) copy-start(bf16[2880,128]{1,0:T(8,128)(2,1)S(1)} %collective-permute-done.4.refs_2_) | copy-start | bytes 2211844
  69.2 24.8 %collective-permute-start.8 = (bf16[2880,128]{1,0:T(8,128)(2,1)S(1)}, bf16[2880,128]{1,0:T(8,128)(2,1)S(1)}, u32[]{:S(2)}, u32[]{:S(2)}) collective-permute-start(bf16[2880,128]{1,0:T(8,128)(2,1)S(1)} %collective-permute-done.4.refs_2_), channel_id=1, source_target_pairs={{0,8},{1,9},{2,10},{3,11},{4,12},{5,13},{6,14},{7,15},{8,24},{9,25... | collective-permute-start | bytes 2211848 | tf_op jit(solution)/shard_map/ppermute | solution.py:316
  95.3 11.2 %collective-permute-start.10 = (bf16[4,4,96,1024]{3,2,1,0:T(8,128)(2,1)S(1)}, bf16[4,4,96,1024]{3,2,1,0:T(8,128)(2,1)}, u32[]{:S(2)}, u32[]{:S(2)}) collective-permute-start(bf16[4,4,96,1024]{3,2,1,0:T(8,128)(2,1)S(1)} %pad_maximum_fusion.even_ref), channel_id=1, source_target_pairs={{0,1},{1,0},{2,3},{3,2},{4,5},{5,4},{6,7},{7,6},{8,9},{9,8},{10,11... | collective-permute-start | bytes 9437192 | tf_op jit(solution)/shard_map/ppermute | solution.py:323
  106.1 6.9 %collective-permute-start.9 = (bf16[4,128,256]{2,1,0:T(8,128)(2,1)}, bf16[4,128,256]{2,1,0:T(8,128)(2,1)S(1)}, u32[]{:S(2)}, u32[]{:S(2)}) collective-permute-start(bf16[4,128,256]{2,1,0:T(8,128)(2,1)} %get-tuple-element.54.key_values_ref), channel_id=1, source_target_pairs={{0,1},{1,2},{2,3},{3,4},{4,5},{5,6},{6,7},{7,0},{8,9},{9,10},{10,1... | collective-permute-start | bytes 786440 | tf_op jit(solution)/shard_map/ppermute | solution.py:320
  121.9 17.8 %collective-permute-start.11 = (bf16[2880,128]{1,0:T(8,128)(2,1)S(1)}, bf16[2880,128]{1,0:T(8,128)(2,1)S(1)}, u32[]{:S(2)}, u32[]{:S(2)}) collective-permute-start(bf16[2880,128]{1,0:T(8,128)(2,1)S(1)} %convert_bitcast_fusion), channel_id=1, source_target_pairs={{0,8},{1,9},{2,10},{3,11},{4,12},{5,13},{6,14},{7,15},{8,24},{9,25... | collective-permute-start | bytes 2211848 | tf_op jit(solution)/shard_map/ppermute | solution.py:316
  139.9 32.7 %copy-start.9 = (bf16[128,2880]{0,1:T(8,128)(2,1)S(1)}, bf16[128,2880]{0,1:T(8,128)(2,1)}, u32[]{:S(2)}) copy-start(bf16[128,2880]{0,1:T(8,128)(2,1)} %param.14) | copy-start | bytes 2211844
  139.9 16.7 %collective-permute-start.12 = (bf16[2880,128]{1,0:T(8,128)(2,1)S(1)}, bf16[2880,128]{1,0:T(8,128)(2,1)S(1)}, u32[]{:S(2)}, u32[]{:S(2)}) collective-permute-start(bf16[2880,128]{1,0:T(8,128)(2,1)S(1)} %fusion.14), channel_id=1, source_target_pairs={{0,8},{1,9},{2,10},{3,11},{4,12},{5,13},{6,14},{7,15},{8,24},{9,25... | collective-permute-start | bytes 2211848 | tf_op jit(solution)/shard_map/ppermute | solution.py:316
  156.8 16.2 %copy-start.18 = (f32[2880]{0:T(1024)S(1)}, f32[2880]{0:T(1024)}, u32[]{:S(2)}) copy-start(f32[2880]{0:T(1024)} %param.18) | copy-start | bytes 34564
  156.8 15.8 %collective-permute-start.13 = (bf16[2880,128]{1,0:T(8,128)(2,1)S(1)}, bf16[2880,128]{1,0:T(8,128)(2,1)S(1)}, u32[]{:S(2)}, u32[]{:S(2)}) collective-permute-start(bf16[2880,128]{1,0:T(8,128)(2,1)S(1)} %fusion.12), channel_id=1, source_target_pairs={{0,8},{1,9},{2,10},{3,11},{4,12},{5,13},{6,14},{7,15},{8,24},{9,25... | collective-permute-start | bytes 2211848 | tf_op jit(solution)/shard_map/ppermute | solution.py:316
  175.2 42.9 %all-to-all-start = ((bf16[32,8,2880]{2,1,0:T(8,128)(2,1)}), bf16[32,8,2880]{2,1,0:T(8,128)(2,1)S(1)}, u32[]{:S(2)}, u32[]{:S(2)}) async-start(bf16[32,8,2880]{2,1,0:T(8,128)(2,1)} %bitcast.33), calls=%async_computation | async-start | bytes 3014656 | tf_op jit(solution)/shard_map/all_to_all | solution.py:501
  219.2 40.2 %all-to-all-start.1 = ((bf16[32,8,2880]{2,1,0:T(8,128)(2,1)}), bf16[32,8,2880]{2,1,0:T(8,128)(2,1)}, u32[]{:S(2)}, u32[]{:S(2)}) async-start(bf16[32,8,2880]{2,1,0:T(8,128)(2,1)} %bitcast.34), calls=%async_computation.1 | async-start | bytes 3014656 | tf_op jit(solution)/shard_map/all_to_all | solution.py:501
  259.4 27.4 %all-to-all-start.2 = ((bf16[32,1,4,2880]{3,2,1,0:T(4,128)(2,1)}), bf16[32,1,4,2880]{3,2,1,0:T(4,128)(2,1)}, u32[]{:S(2)}, u32[]{:S(2)}) async-start(bf16[32,1,4,2880]{3,2,1,0:T(4,128)(2,1)} %bitcast.35), calls=%async_computation.2 | async-start | bytes 1507328 | tf_op jit(solution)/shard_map/all_to_all | solution.py:501
  286.8 42.6 %all-to-all-start.3 = ((bf16[32,8,2880]{2,1,0:T(8,128)(2,1)}), bf16[32,8,2880]{2,1,0:T(8,128)(2,1)S(1)}, u32[]{:S(2)}, u32[]{:S(2)}) async-start(bf16[32,8,2880]{2,1,0:T(8,128)(2,1)} %bitcast.39), calls=%async_computation.3 | async-start | bytes 3014656 | tf_op jit(solution)/shard_map/all_to_all | solution.py:501
  330.5 40.1 %all-to-all-start.4 = ((bf16[32,8,2880]{2,1,0:T(8,128)(2,1)}), bf16[32,8,2880]{2,1,0:T(8,128)(2,1)S(1)}, u32[]{:S(2)}, u32[]{:S(2)}) async-start(bf16[32,8,2880]{2,1,0:T(8,128)(2,1)} %bitcast.41), calls=%async_computation.4 | async-start | bytes 3014656 | tf_op jit(solution)/shard_map/all_to_all | solution.py:501
  353.5 22.4 %copy-start.16 = (bf16[256,256]{1,0:T(8,128)(2,1)S(1)}, bf16[256,256]{1,0:T(8,128)(2,1)}, u32[]{:S(2)}) copy-start(bf16[256,256]{1,0:T(8,128)(2,1)} %get-tuple-element.76) | copy-start | bytes 393220
  371.7 24.0 %all-to-all-start.5 = ((bf16[32,1,4,2880]{3,2,1,0:T(4,128)(2,1)}), bf16[32,1,4,2880]{3,2,1,0:T(4,128)(2,1)}, u32[]{:S(2)}, u32[]{:S(2)}) async-start(bf16[32,1,4,2880]{3,2,1,0:T(4,128)(2,1)} %bitcast.44), calls=%async_computation.5 | async-start | bytes 1507328 | tf_op jit(solution)/shard_map/all_to_all | solution.py:501
  398.0 2.2 copy-start.11
  (13 other events, 18.3 us)
Sparse Core Ops, SparseCore 0:
  9.2 76.1 all-gather.2
